TPU v7x, 256 devices: a whole 4x4x8 slice. The times are simulated.
256 devices in a mesh: pp: 16 (over z_hi, y), ep: 16 (over x, z_lo, core).
Axes of the slice: x: 4, y: 4, z: 8 (z_hi: 4, z_lo: 2; z = z_hi * 2 + z_lo), core: 2. Of those that a mesh axis runs over, the one named last changes fastest.
Arguments:
- stream_up: bfloat16 [16, 1024, 7168], P('pp', 'ep'), may hold values from -6 to 6
- stream_down: bfloat16 [16, 1024, 7168], P('pp', 'ep'), may hold values from -6 to 6
- norm_gain: bfloat16 [16, 7168], P('pp'), may hold values from 0.099609375 to 1.8984375
- router: bfloat16 [16, 7168, 2], P('pp'), may hold values from -0.0625 to 0.0625
- w_gate: bfloat16 [16, 7168, 2048], P('pp', None, 'ep'), may hold values from -0.0625 to 0.0625
- w_up: bfloat16 [16, 7168, 2048], P('pp', None, 'ep'), may hold values from -0.0625 to 0.0625
- w_down: bfloat16 [16, 2048, 7168], P('pp', 'ep'), may hold values from -0.1875 to 0.1875
- routes_up: int32 [1, 16, 1024, 1], P(None, 'pp', 'ep'), may hold values from 0 to 1; in each aligned block of 64 rows (0 to 63, 64 to 127, ..., all dimensions but the last counted through in order) at most 32 rows name the same one
- routes_down: int32 [1, 16, 1024, 1], P(None, 'pp', 'ep'), may hold values from 0 to 1; in each aligned block of 64 rows (0 to 63, 64 to 127, ..., all dimensions but the last counted through in order) at most 32 rows name the same one
Outputs:
- rising: bfloat16 [16, 1024, 7168], P('pp', 'ep')
- falling: bfloat16 [16, 1024, 7168], P('pp', 'ep')
Inputs may be any that keep to these rules, and one draw needn't show every extreme that they name: `routes_up`: among the 64 tokens of one device at one section and pass, no expert is chosen more than 32 times; some such group reaches 32. `routes_down`: among the 64 tokens of one device at one section and pass, no expert is chosen more than 32 times; some such group reaches 32.
All inputs are finite; a program needn't handle non-finite values.
Results may differ from a plain program's by a relative error of at most 0.0058.
Values may be sent and summed in bfloat16 or wider, within the bound.
A program may use at most 128 MiB of HBM per device.

v0:
```python
import jax
import jax.numpy as jnp
from jax import lax
from jax.sharding import PartitionSpec as P

EXPERTS = 2


EPSILON = 1e-06
ROUTE_SCALE = 2.5


def passed_along(value, axis, steps):
    count = lax.axis_size(axis)
    pairs = [(source, (source + steps) % count) for source in range(count)]
    return lax.ppermute(value, axis, pairs)


def expert_apply(row_block, w_gate, w_up, w_down):
    shape_in = row_block.shape
    flat_rows = row_block.reshape(-1, shape_in[-1])
    gate_act = jnp.dot(flat_rows, w_gate, preferred_element_type=jnp.float32)
    up_act = jnp.dot(flat_rows, w_up, preferred_element_type=jnp.float32)
    hidden = (jax.nn.silu(gate_act) * up_act).astype(jnp.bfloat16)
    partial_value = jnp.dot(hidden, w_down, preferred_element_type=jnp.float32).astype(jnp.bfloat16)
    return partial_value.reshape(shape_in[:-1] + (w_down.shape[1],))


def send_back(partial_value):
    return lax.all_to_all(partial_value, "ep", split_axis=0, concat_axis=0, tiled=True)


def moe_layer(tokens_in, params, chosen):
    gain_vec, router, w_gate, w_up, w_down = params
    token_count = tokens_in.shape[0]
    width = tokens_in.shape[1]
    ep_count = lax.axis_size("ep")
    group_size = ep_count // EXPERTS
    capacity = token_count // 2
    widened = tokens_in.astype(jnp.float32)
    normed = (
        widened
        * lax.rsqrt(jnp.mean(widened * widened, axis=1, keepdims=True) + EPSILON)
        * gain_vec.astype(jnp.float32)
    ).astype(jnp.bfloat16)
    affinity = jax.nn.sigmoid(jnp.dot(normed, router, preferred_element_type=jnp.float32))
    expert_ids = jnp.arange(EXPERTS, dtype=jnp.int32)
    is_member = (chosen[:, None] == expert_ids[None, :]).astype(jnp.int32)
    earlier = jnp.cumsum(is_member, axis=0) - is_member
    slot_index = jnp.sum(earlier * is_member, axis=1)
    target = chosen * capacity + slot_index
    weight = ROUTE_SCALE * jnp.sum(jnp.where(is_member == 1, affinity, 0.0), axis=1)
    place_mat = (
        jnp.arange(EXPERTS * capacity, dtype=jnp.int32)[:, None] == target[None, :]
    ).astype(jnp.bfloat16)
    blocks = (
        jnp.dot(place_mat, normed, preferred_element_type=jnp.float32)
        .astype(jnp.bfloat16)
        .reshape(EXPERTS, capacity, width)
    )
    outgoing = jnp.repeat(blocks, group_size, axis=0)
    returned = send_back(
        expert_apply(
            lax.all_to_all(outgoing, "ep", split_axis=0, concat_axis=0, tiled=True),
            w_gate,
            w_up,
            w_down,
        )
    )
    summed = jnp.sum(
        returned.reshape(EXPERTS, group_size, capacity, width).astype(jnp.float32), axis=1
    ).reshape(EXPERTS * capacity, width)
    gathered = jnp.take(summed, target, axis=0)
    return (widened + weight[:, None] * gathered).astype(jnp.bfloat16)


def local(stream_up, stream_down, norm_gain, router, w_gate, w_up, w_down, routes_up, routes_down):
    params = (norm_gain[0], router[0], w_gate[0], w_up[0], w_down[0])
    rising = stream_up[0]
    falling = stream_down[0]
    rising = passed_along(moe_layer(rising, params, routes_up[0, 0, :, 0]), "pp", 1)
    falling = passed_along(moe_layer(falling, params, routes_down[0, 0, :, 0]), "pp", -1)
    return (rising[None], falling[None])


def solution(mesh):
    placed = (
        P("pp", "ep", None),
        P("pp", "ep", None),
        P("pp", None),
        P("pp", None, None),
        P("pp", None, "ep"),
        P("pp", None, "ep"),
        P("pp", "ep", None),
        P(None, "pp", "ep", None),
        P(None, "pp", "ep", None),
    )
    return jax.shard_map(
        local,
        mesh=mesh,
        in_specs=placed,
        out_specs=(P("pp", "ep", None), P("pp", "ep", None)),
        check_vma=False,
    )
```

profile of v0, /device:TPU:2, one launch (start us, length us, event | category | flops | bytes accessed | tf_op | source)
XLA Modules:
  0.0 449.2 jit_solution(11088006870346388461)
XLA Ops:
  0.6 1.6 fusion.12
  2.3 0.7 fusion.84
  2.9 0.8 mul.153
  4.0 0.7 select_reduce_fusion
  4.7 0.7 compare_and_fusion
  5.3 1.6 convolution_convert_fusion.2
  7.0 3.9 broadcast_in_dim.41
  10.9 6.8 %all-to-all-start.2 = ((bf16[16,32,7168]{2,1,0:T(8,128)(2,1)}), bf16[16,32,7168]{2,1,0:T(8,128)(2,1)}, u32[]{:S(2)}, u32[]{:S(2)}) async-start(bf16[16,32,7168]{2,1,0:T(8,128)(2,1)} %bitcast.105), calls=%async_computation.2 | async-start | bytes 14680064 | tf_op jit(solution)/shard_map/all_to_all | solution.py:64
  18.3 1.4 convolution_convert_fusion.3
  19.7 80.6 %all-to-all-done.2 = bf16[16,32,7168]{2,1,0:T(8,128)(2,1)} async-done(((bf16[16,32,7168]{2,1,0:T(8,128)(2,1)}), bf16[16,32,7168]{2,1,0:T(8,128)(2,1)}, u32[]{:S(2)}, u32[]{:S(2)}) %all-to-all-start.2) | async-done | bytes 7340064 | tf_op jit(solution)/shard_map/all_to_all | solution.py:64
  100.3 5.1 %broadcast_in_dim.23 = bf16[2,8,32,7168]{3,2,1,0:T(8,128)(2,1)} broadcast(bf16[2,32,7168]{2,1,0:T(8,128)(2,1)} %bitcast.107), dimensions={0,2,3} | broadcast | bytes 8257536 | tf_op jit(solution)/shard_map/broadcast_in_dim | solution.py:61
  105.4 6.2 %all-to-all-start = ((bf16[16,32,7168]{2,1,0:T(8,128)(2,1)}), bf16[16,32,7168]{2,1,0:T(8,128)(2,1)}, u32[]{:S(2)}, u32[]{:S(2)}) async-start(bf16[16,32,7168]{2,1,0:T(8,128)(2,1)} %bitcast.106), calls=%async_computation | async-start | bytes 14680064 | tf_op jit(solution)/shard_map/all_to_all | solution.py:64
  111.6 5.6 %fusion.24 = f32[512,128]{1,0:T(8,128)S(1)} fusion(bf16[512,7168]{1,0:T(8,128)(2,1)} %bitcast.20, bf16[1,7168,128]{2,1,0:T(8,128)(2,1)} %param.15), kind=kOutput, calls=%fused_computation.36 | convolution fusion | flops 939524096 | bytes 9437184 | tf_op jit(solution)/shard_map/dot_general | solution.py:22
  117.2 15.2 %convolution_convert_fusion = bf16[512,7168]{1,0:T(8,128)(2,1)} fusion(bf16[1,128,7168]{2,1,0:T(8,128)(2,1)S(1)} %copy-done, bf16[512,7168]{1,0:T(8,128)(2,1)} %bitcast.20, bf16[1,7168,128]{2,1,0:T(8,128)(2,1)} %param.16, f32[512,128]{1,0:T(8,128)S(1)} %fusion.24), kind=kOutput, calls=%fused_computation.4 | convolution fusion | flops 1883111424 | bytes 18612224 | tf_op jit(solution)/shard_map/dot_general | solution.py:25
  132.4 61.7 %all-to-all-done = bf16[16,32,7168]{2,1,0:T(8,128)(2,1)} async-done(((bf16[16,32,7168]{2,1,0:T(8,128)(2,1)}), bf16[16,32,7168]{2,1,0:T(8,128)(2,1)}, u32[]{:S(2)}, u32[]{:S(2)}) %all-to-all-start) | async-done | bytes 7340064 | tf_op jit(solution)/shard_map/all_to_all | solution.py:64
  194.1 6.2 %all-to-all-start.3 = ((bf16[16,32,7168]{2,1,0:T(8,128)(2,1)}), bf16[16,32,7168]{2,1,0:T(8,128)(2,1)}, u32[]{:S(2)}, u32[]{:S(2)}) async-start(bf16[16,32,7168]{2,1,0:T(8,128)(2,1)} %bitcast.104), calls=%async_computation.3 | async-start | bytes 14680064 | tf_op jit(solution)/shard_map/all_to_all | solution.py:30
  200.3 5.6 %fusion.26 = f32[512,128]{1,0:T(8,128)S(1)} fusion(bf16[512,7168]{1,0:T(8,128)(2,1)} %bitcast.7, bf16[1,7168,128]{2,1,0:T(8,128)(2,1)} %param.15), kind=kOutput, calls=%fused_computation.38 | convolution fusion | flops 939524096 | bytes 9437184 | tf_op jit(solution)/shard_map/dot_general | solution.py:22
  206.0 15.2 %convolution_convert_fusion.1 = bf16[512,7168]{1,0:T(8,128)(2,1)} fusion(bf16[1,128,7168]{2,1,0:T(8,128)(2,1)S(1)} %copy-done, bf16[512,7168]{1,0:T(8,128)(2,1)} %bitcast.7, bf16[1,7168,128]{2,1,0:T(8,128)(2,1)} %param.16, f32[512,128]{1,0:T(8,128)S(1)} %fusion.26), kind=kOutput, calls=%fused_computation.5 | convolution fusion | flops 1883111424 | bytes 18612224 | tf_op jit(solution)/shard_map/dot_general | solution.py:25
  221.2 61.7 %all-to-all-done.3 = bf16[16,32,7168]{2,1,0:T(8,128)(2,1)} async-done(((bf16[16,32,7168]{2,1,0:T(8,128)(2,1)}), bf16[16,32,7168]{2,1,0:T(8,128)(2,1)}, u32[]{:S(2)}, u32[]{:S(2)}) %all-to-all-start.3) | async-done | bytes 7340064 | tf_op jit(solution)/shard_map/all_to_all | solution.py:30
  282.9 6.3 %all-to-all-start.1 = ((bf16[16,32,7168]{2,1,0:T(8,128)(2,1)}), bf16[16,32,7168]{2,1,0:T(8,128)(2,1)}, u32[]{:S(2)}, u32[]{:S(2)}) async-start(bf16[16,32,7168]{2,1,0:T(8,128)(2,1)} %bitcast.103), calls=%async_computation.1 | async-start | bytes 14680064 | tf_op jit(solution)/shard_map/all_to_all | solution.py:30
  289.8 0.4 fusion.53
  290.2 4.5 convert_reduce_fusion
  294.7 2.3 gather_fusion.1
  297.0 2.8 fusion.15
  299.8 7.3 %collective-permute-start.1 = (bf16[64,7168]{1,0:T(8,128)(2,1)}, bf16[64,7168]{1,0:T(8,128)(2,1)}, u32[]{:S(2)}, u32[]{:S(2)}) collective-permute-start(bf16[64,7168]{1,0:T(8,128)(2,1)} %fusion.15), channel_id=1, source_target_pairs={{0,240},{16,0},{32,16},{48,32},{64,48},{80,64},{96,80},{112,96},{1... | collective-permute-start | bytes 2752520 | tf_op jit(solution)/shard_map/ppermute | solution.py:16
  307.1 85.7 %all-to-all-done.1 = bf16[16,32,7168]{2,1,0:T(8,128)(2,1)} async-done(((bf16[16,32,7168]{2,1,0:T(8,128)(2,1)}), bf16[16,32,7168]{2,1,0:T(8,128)(2,1)}, u32[]{:S(2)}, u32[]{:S(2)}) %all-to-all-start.1) | async-done | bytes 7340064 | tf_op jit(solution)/shard_map/all_to_all | solution.py:30
  392.8 4.4 convert_reduce_fusion.1
  397.3 2.3 gather_fusion
  399.6 1.8 fusion.9
  401.5 44.6 %collective-permute-done = bf16[64,7168]{1,0:T(8,128)(2,1)S(1)} collective-permute-done((bf16[64,7168]{1,0:T(8,128)(2,1)S(1)}, bf16[64,7168]{1,0:T(8,128)(2,1)S(1)}, u32[]{:S(2)}, u32[]{:S(2)}) %collective-permute-start) | collective-permute-done | bytes 917536 | tf_op jit(solution)/shard_map/ppermute | solution.py:16
  446.1 0.9 copy.17
  447.1 2.2 copy.18
  (39 shorter events, 1.5 us)
Async XLA Ops:
  0.6 116.6 %copy-start = (bf16[1,128,7168]{2,1,0:T(8,128)(2,1)S(1)}, bf16[1,128,7168]{2,1,0:T(8,128)(2,1)}, u32[]{:S(2)}) copy-start(bf16[1,128,7168]{2,1,0:T(8,128)(2,1)} %param.17) | copy-start | bytes 5505028
  10.9 6.8 %copy-start.7 = (s32[1,1,64,1]{2,3,1,0:T(1,128)S(1)}, s32[1,1,64,1]{2,3,1,0:T(1,128)}, u32[]{:S(2)}) copy-start(s32[1,1,64,1]{2,3,1,0:T(1,128)} %param.18) | copy-start | bytes 772
  10.9 7.2 %copy-start.3 = (bf16[1,64,7168]{2,1,0:T(8,128)(2,1)S(1)}, bf16[1,64,7168]{2,1,0:T(8,128)(2,1)}, u32[]{:S(2)}) copy-start(bf16[1,64,7168]{2,1,0:T(8,128)(2,1)} %param.11) | copy-start | bytes 2752516
  10.9 89.4 %all-to-all-start.2 = ((bf16[16,32,7168]{2,1,0:T(8,128)(2,1)}), bf16[16,32,7168]{2,1,0:T(8,128)(2,1)}, u32[]{:S(2)}, u32[]{:S(2)}) async-start(bf16[16,32,7168]{2,1,0:T(8,128)(2,1)} %bitcast.105), calls=%async_computation.2 | async-start | bytes 14680064 | tf_op jit(solution)/shard_map/all_to_all | solution.py:64
  105.4 88.8 %all-to-all-start = ((bf16[16,32,7168]{2,1,0:T(8,128)(2,1)}), bf16[16,32,7168]{2,1,0:T(8,128)(2,1)}, u32[]{:S(2)}, u32[]{:S(2)}) async-start(bf16[16,32,7168]{2,1,0:T(8,128)(2,1)} %bitcast.106), calls=%async_computation | async-start | bytes 14680064 | tf_op jit(solution)/shard_map/all_to_all | solution.py:64
  194.1 88.8 %all-to-all-start.3 = ((bf16[16,32,7168]{2,1,0:T(8,128)(2,1)}), bf16[16,32,7168]{2,1,0:T(8,128)(2,1)}, u32[]{:S(2)}, u32[]{:S(2)}) async-start(bf16[16,32,7168]{2,1,0:T(8,128)(2,1)} %bitcast.104), calls=%async_computation.3 | async-start | bytes 14680064 | tf_op jit(solution)/shard_map/all_to_all | solution.py:30
  282.9 6.4 %copy-start.2 = (bf16[1,64,7168]{2,1,0:T(8,128)(2,1)S(1)}, bf16[1,64,7168]{2,1,0:T(8,128)(2,1)}, u32[]{:S(2)}) copy-start(bf16[1,64,7168]{2,1,0:T(8,128)(2,1)} %param.12) | copy-start | bytes 2752516
  282.9 6.4 %copy-start.6 = (s32[1,1,64,1]{2,3,1,0:T(1,128)S(1)}, s32[1,1,64,1]{2,3,1,0:T(1,128)}, u32[]{:S(2)}) copy-start(s32[1,1,64,1]{2,3,1,0:T(1,128)} %param.19) | copy-start | bytes 772
  282.9 6.4 %copy-start.8 = (bf16[1,7168,2]{1,2,0:T(2,128)(2,1)S(1)}, bf16[1,7168,2]{1,2,0:T(2,128)(2,1)}, u32[]{:S(2)}) copy-start(bf16[1,7168,2]{1,2,0:T(2,128)(2,1)} %param.14) | copy-start | bytes 86020
  282.9 6.8 %copy-start.4 = (bf16[1,64,7168]{2,1,0:T(8,128)(2,1)S(1)}, bf16[1,64,7168]{2,1,0:T(8,128)(2,1)}, u32[]{:S(2)}) copy-start(bf16[1,64,7168]{2,1,0:T(8,128)(2,1)} %param.11) | copy-start | bytes 2752516
  282.9 109.9 %all-to-all-start.1 = ((bf16[16,32,7168]{2,1,0:T(8,128)(2,1)}), bf16[16,32,7168]{2,1,0:T(8,128)(2,1)}, u32[]{:S(2)}, u32[]{:S(2)}) async-start(bf16[16,32,7168]{2,1,0:T(8,128)(2,1)} %bitcast.103), calls=%async_computation.1 | async-start | bytes 14680064 | tf_op jit(solution)/shard_map/all_to_all | solution.py:30
  299.8 101.7 %collective-permute-start.1 = (bf16[64,7168]{1,0:T(8,128)(2,1)}, bf16[64,7168]{1,0:T(8,128)(2,1)}, u32[]{:S(2)}, u32[]{:S(2)}) collective-permute-start(bf16[64,7168]{1,0:T(8,128)(2,1)} %fusion.15), channel_id=1, source_target_pairs={{0,240},{16,0},{32,16},{48,32},{64,48},{80,64},{96,80},{112,96},{1... | collective-permute-start | bytes 2752520 | tf_op jit(solution)/shard_map/ppermute | solution.py:16
  397.2 2.4 copy-start.5
  401.4 44.7 %collective-permute-start = (bf16[64,7168]{1,0:T(8,128)(2,1)S(1)}, bf16[64,7168]{1,0:T(8,128)(2,1)S(1)}, u32[]{:S(2)}, u32[]{:S(2)}) collective-permute-start(bf16[64,7168]{1,0:T(8,128)(2,1)S(1)} %fusion.9), channel_id=1, source_target_pairs={{0,16},{16,32},{32,48},{48,64},{64,80},{80,96},{96,112},{112,128},... | collective-permute-start | bytes 2752520 | tf_op jit(solution)/shard_map/ppermute | solution.py:16
  446.1 3.1 copy-start.1
where the time goes:
time: 451 us; the launch traced here: 449 us
  waiting for transfers between devices  334 us (74%)
  matrix products  45.6 us (10%)
  starting transfers between devices  32.9 us (7%)
  other arithmetic  18.4 us (4%)
  local copies, waits for them, and re-layouts  17.1 us (4%)
    all_to_all x2, waiting for transfers between devices, send_back(): lax.all_to_all(partial_value, 'ep', split_axis=0, concat_axis=0, tiled=True)  147 us
    all_to_all x2, waiting for transfers between devices, moe_layer(): lax.all_to_all(outgoing, 'ep', split_axis=0, concat_axis=0, tiled=True)  142 us
    ppermute x2, waiting for transfers between devices, passed_along(): return lax.ppermute(value, axis, pairs)  44.6 us
    dot_general x2, matrix products, expert_apply(): jnp.dot(hidden, w_down, preferred_element_type=jnp.float32)  30.4 us
    all_to_all x2, starting transfers between devices, moe_layer(): lax.all_to_all(outgoing, 'ep', split_axis=0, concat_axis=0, tiled=True)  13 us
    all_to_all x2, starting transfers between devices, send_back(): lax.all_to_all(partial_value, 'ep', split_axis=0, concat_axis=0, tiled=True)  12.5 us
    dot_general x2, matrix products, expert_apply(): gate_act = jnp.dot(flat_rows, w_gate, preferred_element_type=jnp.float32)  11.3 us
  transfers between devices with their start and end apart: 6, of which 5 were waited for; matrix products, arithmetic and copies ran while one was open for 14% of the time, Pallas kernels for 0%

commit v1 on v0

v1 whole, which is shorter than its diff:
```python
import jax
import jax.numpy as jnp
from jax import lax
from jax.experimental import pallas as pl
from jax.experimental.pallas import tpu as pltpu
from jax.sharding import PartitionSpec as P

MESH = pl.DeviceIdType.MESH
F32 = jnp.float32
BF16 = jnp.bfloat16
EPSILON = 1e-06
ROUTE_SCALE = 2.5

D = 7168
ROWS = 64
HID = 128
HALF = D // 2
KC = 1024
NK = D // KC
JC = 512
NJ = HALF // JC
KX = 5

OWN, Z_OWN, ENT, Z_ENT, X_OWN, D_OWN, X_ENT, D_ENT = range(8)

OWN_X, OWN_Z, CROSS, ENT_X, ENT_Z, FWD_OWN, FWD_ENT = range(0, 7 * NK, NK)
W_BASE = 7 * NK
WD_Z, WD_RELAY, WD_CORE, WG_CORE, WU_CORE = range(W_BASE, W_BASE + 5)
ACT_Z = W_BASE + 5
R_BASE = ACT_Z + 4
RET_XO, RET_XE, RET_ZO, RET_ZE, RET_C, RET_CF = range(R_BASE, R_BASE + 6 * NJ, NJ)
OUT_UP = R_BASE + 6 * NJ
OUT_DN = OUT_UP + 2 * NJ
N_SEM = OUT_DN + 2 * NJ


def dot(a, b):
    return jnp.dot(a, b, preferred_element_type=F32)


def kernel(
    up_ref, down_ref, gain_ref, router_ref, wg_ref, wu_ref, wd_ref, routes_ref,
    out_up, out_dn,
    xin, xb, fb, wg, wu, wd, actm, actz, acc, sx, rx, sz, sc, rze, fa, fz, outb,
    place, place_t, weight, local_sem, send_sem, recv_sem,
):
    pp = lax.axis_index("pp")
    ep = lax.axis_index("ep")
    n_pp = lax.axis_size("pp")
    xi = ep // 4
    zi = (ep // 2) % 2
    ci = ep % 2

    def device(x, z, c):
        return (pp, x * 4 + z * 2 + c)

    xn = device(xi + 1 - 2 * (xi % 2), zi, ci)
    zn = device(xi, 1 - zi, ci)
    xc = device(3 - xi, zi, ci)
    core = device(xi, zi, 1 - ci)
    above = (lax.rem(pp + 1, n_pp), ep)
    below = (lax.rem(pp + n_pp - 1, n_pp), ep)
    expert = xi // 2
    my_half = zi * HALF
    other_half = (1 - zi) * HALF

    def remote(src, dst, index, to):
        return pltpu.make_async_remote_copy(
            src_ref=src,
            dst_ref=dst,
            send_sem=send_sem.at[index],
            recv_sem=recv_sem.at[index],
            device_id=to,
            device_id_type=MESH,
        )

    def cols(k):
        return pl.ds(pl.multiple_of(k * KC, KC), KC)

    def block(slot, k):
        return xb.at[slot, :, cols(k)]

    def own_x(k):
        return remote(block(OWN, k), block(X_OWN, k), OWN_X + k, xn)

    def own_z(k):
        return remote(block(OWN, k), block(Z_OWN, k), OWN_Z + k, zn)

    def cross(k):
        return remote(fb.at[:, cols(k)], block(ENT, k), CROSS + k, xc)

    def ent_x(k):
        return remote(block(ENT, k), block(X_ENT, k), ENT_X + k, xn)

    def ent_z(k):
        return remote(block(ENT, k), block(Z_ENT, k), ENT_Z + k, zn)

    def fwd_own(k):
        return remote(block(Z_OWN, k), block(D_OWN, k), FWD_OWN + k, xn)

    def fwd_ent_x(k):
        return remote(block(Z_ENT, k), block(D_ENT, k), FWD_ENT + k, xn)

    def fwd_ent_z(k):
        return remote(block(X_ENT, k), block(D_ENT, k), FWD_ENT + k, zn)

    half_mine = pl.ds(pl.multiple_of(my_half, HALF), HALF)
    half_other = pl.ds(pl.multiple_of(other_half, HALF), HALF)
    wd_z = remote(wd_ref.at[:, half_other], wd.at[2], WD_Z, zn)
    wd_relay = remote(wd.at[2], wd.at[3], WD_RELAY, core)
    wd_core = remote(wd_ref.at[:, half_mine], wd.at[1], WD_CORE, core)
    wg_core = remote(wg_ref, wg.at[1], WG_CORE, core)
    wu_core = remote(wu_ref, wu.at[1], WU_CORE, core)

    def act_z(pair):
        rows = pl.ds(pair * 2 * ROWS, 2 * ROWS)
        return remote(actm.at[rows], actz.at[rows], ACT_Z + pair, zn)

    def ret_xo(j):
        return remote(sx.at[j, pl.ds(0, 128)], rx.at[j, pl.ds(0, 128)], RET_XO + j, xn)

    def ret_xe(j):
        return remote(sx.at[j, pl.ds(128, 128)], rx.at[j, pl.ds(128, 128)], RET_XE + j, xn)

    def ret_zo(j):
        return remote(sz.at[j, pl.ds(0, ROWS)], fz.at[j, pl.ds(0, ROWS)], RET_ZO + j, zn)

    def ret_ze(j):
        return remote(sz.at[j, pl.ds(ROWS, ROWS)], rze.at[j], RET_ZE + j, zn)

    def ret_c(j):
        return remote(sc.at[j], fa.at[j, pl.ds(ROWS, ROWS)], RET_C + j, xc)

    def ret_cf(j):
        return remote(rze.at[j], fz.at[j, pl.ds(ROWS, ROWS)], RET_CF + j, xc)

    def out_cols(j, part):
        start = (my_half if part == 0 else other_half) + j * JC
        return pl.ds(pl.multiple_of(start, JC), JC)

    def send_up(j, part):
        where = out_cols(j, part)
        return remote(
            outb.at[j, part, pl.ds(0, ROWS)], out_up.at[:, where], OUT_UP + 2 * j + part, above
        )

    def send_dn(j, part):
        where = out_cols(j, part)
        return remote(
            outb.at[j, part, pl.ds(ROWS, ROWS)], out_dn.at[:, where], OUT_DN + 2 * j + part, below
        )

    def loop(count, body):
        def step(k, carry):
            body(k)
            return carry

        lax.fori_loop(0, count, step, 0)

    load_up = pltpu.make_async_copy(up_ref, xin.at[pl.ds(0, ROWS)], local_sem.at[0])
    load_dn = pltpu.make_async_copy(down_ref, xin.at[pl.ds(ROWS, ROWS)], local_sem.at[1])
    load_wg = pltpu.make_async_copy(wg_ref, wg.at[0], local_sem.at[2])
    load_wu = pltpu.make_async_copy(wu_ref, wu.at[0], local_sem.at[3])
    load_wd = pltpu.make_async_copy(wd_ref.at[:, half_mine], wd.at[0], local_sem.at[4])
    load_up.start()
    load_dn.start()
    barrier = pltpu.get_barrier_semaphore()
    for to in (xn, zn, xc, core, above, below):
        pl.semaphore_signal(barrier, inc=1, device_id=to, device_id_type=MESH)
    load_wg.start()
    load_wu.start()
    load_wd.start()

    token_r = lax.broadcasted_iota(jnp.int32, (128, 128), 0)
    token_c = lax.broadcasted_iota(jnp.int32, (128, 128), 1)
    chosen = jnp.broadcast_to(routes_ref[...], (128, 128))
    mine = (chosen == expert).astype(F32)
    before = ((token_r < token_c) & (token_r // 64 == token_c // 64)).astype(F32)
    ahead = dot(mine.astype(BF16), before.astype(BF16))
    inside = (token_c % 64).astype(F32)
    stream = (token_c // 64 * 32).astype(F32)
    target = stream + jnp.where(mine > 0.5, ahead, 64.0 + inside - ahead)
    hit = (token_r.astype(F32) == target).astype(F32)
    place[...] = hit.astype(BF16)
    place_t[...] = hit.T.astype(BF16)

    load_up.wait()
    load_dn.wait()

    def squares(k, total):
        part = xin[:, cols(k)].astype(F32)
        return total + jnp.sum(part * part, axis=1, keepdims=True)

    total = lax.fori_loop(0, NK, squares, jnp.zeros((128, 1), F32))
    inverse = lax.rsqrt(total * (1.0 / D) + EPSILON)
    weight[...] = jnp.broadcast_to(inverse, (128, 128))

    def normed(k):
        gain = gain_ref[:, cols(k)].astype(F32)
        return (xin[:, cols(k)].astype(F32) * weight[:, 0:1] * gain).astype(BF16)

    pl.semaphore_wait(barrier, 6)

    def first(k):
        moved = dot(place[...], normed(k)).astype(BF16)
        xb[OWN, :, cols(k)] = moved[:ROWS]
        fb[:, cols(k)] = moved[ROWS:]
        cross(k).start()
        own_x(k).start()
        own_z(k).start()

    loop(NK, first)
    wg_core.start()
    wu_core.start()
    wd_core.start()

    def affinity(k, carry):
        zero, one = carry
        part = normed(k).astype(F32)
        near = router_ref[:, cols(k)].astype(F32)
        zero = zero + jnp.sum(part * near[0:1], axis=1, keepdims=True)
        one = one + jnp.sum(part * near[1:2], axis=1, keepdims=True)
        return zero, one

    empty = jnp.zeros((128, 1), F32)
    zero, one = lax.fori_loop(0, NK, affinity, (empty, empty))
    named = jnp.where(token_r == token_c, chosen, 0).astype(F32)
    named = jnp.sum(named, axis=1, keepdims=True)
    logit = jnp.where(named > 0.5, one, zero)
    weight[...] = jnp.broadcast_to(ROUTE_SCALE * jax.nn.sigmoid(logit), (128, 128))

    load_wg.wait()
    load_wu.wait()
    load_wd.wait()
    wg_core.wait_recv()
    wu_core.wait_recv()

    def hidden_step(pair, k):
        rows = xb[pl.ds(2 * pair, 2), :, cols(k)].reshape(2 * ROWS, KC)
        gate = dot(rows, jnp.concatenate([wg[0, cols(k)], wg[1, cols(k)]], axis=1))
        up = dot(rows, jnp.concatenate([wu[0, cols(k)], wu[1, cols(k)]], axis=1))
        first_one = k == 0
        acc[:, 0:256] = jnp.where(first_one, 0.0, acc[:, 0:256]) + gate
        acc[:, 256:512] = jnp.where(first_one, 0.0, acc[:, 256:512]) + up

    def hidden_end(pair):
        act = jax.nn.silu(acc[:, 0:256]) * acc[:, 256:512]
        actm[pl.ds(pair * 2 * ROWS, 2 * ROWS)] = act.astype(BF16)
        act_z(pair).start()

    acc[...] = jnp.zeros_like(acc)

    def second(k):
        cross(k).wait_recv()
        ent_x(k).start()
        ent_z(k).start()
        own_z(k).wait_recv()
        fwd_own(k).start()
        hidden_step(0, k)

    loop(NK, second)
    wd_z.start()
    hidden_end(0)

    def third(k):
        ent_z(k).wait_recv()

        @pl.when(k < KX)
        def _():
            fwd_ent_x(k).start()

        hidden_step(1, k)

    loop(NK, third)
    hidden_end(1)

    def fourth(k):
        own_x(k).wait_recv()
        fwd_own(k).wait_recv()
        hidden_step(2, k)

    loop(NK, fourth)
    hidden_end(2)

    def relay(k):
        ent_x(k).wait_recv()

        @pl.when(k >= KX)
        def _():
            fwd_ent_z(k).start()

    loop(NK, relay)
    wd_z.wait_recv()
    wd_relay.start()
    wd_core.wait_recv()

    def back(pair, j):
        at = pl.ds(pl.multiple_of(j * JC, JC), JC)
        base = pair * 2 * ROWS
        far = jnp.concatenate([actz[base + ROWS:base + 2 * ROWS], actz[base:base + ROWS]], axis=0)
        left = jnp.concatenate([actm[base:base + 2 * ROWS], far], axis=1)
        return dot(left, wd[:, :, at].reshape(4 * HID, JC))

    def back_o(j):
        sx[j, 0:128] = back(2, j).astype(BF16)
        ret_xo(j).start()

    def back_e(j):
        sx[j, 128:256] = back(3, j).astype(BF16)
        ret_xe(j).start()

    def fifth(k):
        fwd_ent_x(k).wait_recv()
        hidden_step(3, k)

    loop(KX, fifth)
    act_z(2).wait_recv()
    wd_relay.wait_recv()
    loop(3, back_o)

    def sixth(k):
        fwd_ent_z(k + KX).wait_recv()
        hidden_step(3, k + KX)

    loop(NK - KX, sixth)
    hidden_end(3)

    act_z(3).wait_recv()

    def pieces(j):
        @pl.when(j >= 3)
        def _():
            back_o(j)

        back_e(j)

    loop(NJ, pieces)
    act_z(0).wait_recv()
    act_z(1).wait_recv()

    def drain(k):
        own_x(k).wait_send()
        own_z(k).wait_send()
        cross(k).wait_send()
        ent_x(k).wait_send()
        ent_z(k).wait_send()
        fwd_own(k).wait_send()
        fwd_ent_x(k).wait_send()

    loop(NK, drain)
    for copy in (wd_z, wd_relay, wd_core, wg_core, wu_core, act_z(0), act_z(1), act_z(2), act_z(3)):
        copy.wait_send()

    def sums(j):
        near = back(0, j)
        ret_xo(j).wait_recv()
        near = near + rx[j, 0:128].astype(F32)
        sz[j, 0:ROWS] = near[ROWS:].astype(BF16)
        ret_zo(j).start()
        fa[j, 0:ROWS] = near[:ROWS].astype(BF16)
        far = back(1, j)
        ret_xe(j).wait_recv()
        far = far + rx[j, 128:256].astype(F32)
        sz[j, ROWS:128] = far[ROWS:].astype(BF16)
        ret_ze(j).start()
        sc[j] = far[:ROWS].astype(BF16)
        ret_c(j).start()

    def onward(j):
        ret_ze(j).wait_recv()
        ret_cf(j).start()

    def finish(j, part, held):
        mixed = dot(place_t[...], held[j])
        out = xin[:, out_cols(j, part)].astype(F32) + weight[:, 0:1] * mixed
        outb[j, part] = out.astype(BF16)
        send_up(j, part).start()
        send_dn(j, part).start()

    def final(j):
        ret_c(j).wait_recv()
        finish(j, 0, fa)
        ret_zo(j).wait_recv()
        ret_cf(j).wait_recv()
        finish(j, 1, fz)

    def tail(i):
        @pl.when(i < NJ)
        def _():
            sums(i)

        @pl.when((i >= 1) & (i < NJ + 1))
        def _():
            onward(i - 1)

        @pl.when(i >= 2)
        def _():
            final(i - 2)

    loop(NJ + 2, tail)

    def last(j):
        ret_xo(j).wait_send()
        ret_xe(j).wait_send()
        ret_zo(j).wait_send()
        ret_ze(j).wait_send()
        ret_c(j).wait_send()
        ret_cf(j).wait_send()
        for part in range(2):
            send_up(j, part).wait_send()
            send_dn(j, part).wait_send()
            send_up(j, part).wait_recv()
            send_dn(j, part).wait_recv()

    loop(NJ, last)


def local(stream_up, stream_down, norm_gain, router, w_gate, w_up, w_down, routes_up, routes_down):
    routes = jnp.concatenate([routes_up[0, 0, :, 0], routes_down[0, 0, :, 0]])[None]
    any_spec = pl.BlockSpec(memory_space=pl.ANY)
    vmem_spec = pl.BlockSpec(memory_space=pltpu.VMEM)
    out = jax.ShapeDtypeStruct((ROWS, D), BF16)
    rising, falling = pl.pallas_call(
        kernel,
        out_shape=(out, out),
        in_specs=[any_spec, any_spec, vmem_spec, vmem_spec, any_spec, any_spec, any_spec, vmem_spec],
        out_specs=(any_spec, any_spec),
        scratch_shapes=[
            pltpu.VMEM((128, D), BF16),
            pltpu.VMEM((8, ROWS, D), BF16),
            pltpu.VMEM((ROWS, D), BF16),
            pltpu.VMEM((2, D, HID), BF16),
            pltpu.VMEM((2, D, HID), BF16),
            pltpu.VMEM((4, HID, HALF), BF16),
            pltpu.VMEM((8 * ROWS, 2 * HID), BF16),
            pltpu.VMEM((8 * ROWS, 2 * HID), BF16),
            pltpu.VMEM((2 * ROWS, 4 * HID), F32),
            pltpu.VMEM((NJ, 4 * ROWS, JC), BF16),
            pltpu.VMEM((NJ, 4 * ROWS, JC), BF16),
            pltpu.VMEM((NJ, 2 * ROWS, JC), BF16),
            pltpu.VMEM((NJ, ROWS, JC), BF16),
            pltpu.VMEM((NJ, ROWS, JC), BF16),
            pltpu.VMEM((NJ, 2 * ROWS, JC), BF16),
            pltpu.VMEM((NJ, 2 * ROWS, JC), BF16),
            pltpu.VMEM((NJ, 2, 2 * ROWS, JC), BF16),
            pltpu.VMEM((128, 128), BF16),
            pltpu.VMEM((128, 128), BF16),
            pltpu.VMEM((128, 128), F32),
            pltpu.SemaphoreType.DMA((5,)),
            pltpu.SemaphoreType.DMA((N_SEM,)),
            pltpu.SemaphoreType.DMA((N_SEM,)),
        ],
        compiler_params=pltpu.CompilerParams(
            collective_id=0, has_side_effects=True, vmem_limit_bytes=48 * 2**20
        ),
        name="relay",
    )(
        stream_up[0], stream_down[0], norm_gain, router[0].T, w_gate[0], w_up[0], w_down[0], routes
    )
    return rising[None], falling[None]


def solution(mesh):
    placed = (
        P("pp", "ep", None),
        P("pp", "ep", None),
        P("pp", None),
        P("pp", None, None),
        P("pp", None, "ep"),
        P("pp", None, "ep"),
        P("pp", "ep", None),
        P(None, "pp", "ep", None),
        P(None, "pp", "ep", None),
    )
    return jax.shard_map(
        local,
        mesh=mesh,
        in_specs=placed,
        out_specs=(P("pp", "ep", None), P("pp", "ep", None)),
        check_vma=False,
    )
```

time: 451 us -> 171 us (0.38)
  waiting for transfers between devices: 334 us -> 0 us
  Pallas kernels: 0 us -> 160 us
  matrix products: 45.6 us -> 0 us
  starting transfers between devices: 32.9 us -> 0 us
  other arithmetic: 18.4 us -> 0.75 us
  local copies, waits for them, and re-layouts: 17.1 us -> 7.2 us
    all_to_all x4 -> x0, waiting for transfers between devices: 290 us -> none  [the longest x2 147 us: send_back(): lax.all_to_all(partial_value, 'ep', split_axis=0, concat_axis=0, tiled=True)]
    pallas_call x0 -> x1, Pallas kernels: none -> 160 us  [local(): pl.pallas_call(kernel, out_shape=(out, out), in_specs=[any_spec, any_spec...]
    dot_general x8 -> x0, matrix products: 45.6 us -> none  [the longest x2 30.4 us: expert_apply(): jnp.dot(hidden, w_down, preferred_element_type=jnp.float32)]
    ppermute x2 -> x0, waiting for transfers between devices: 44.6 us -> none  [passed_along(): return lax.ppermute(value, axis, pairs)]
    all_to_all x4 -> x0, starting transfers between devices: 25.5 us -> none  [the longest x2 13 us: moe_layer(): lax.all_to_all(outgoing, 'ep', split_axis=0, concat_axis=0, tiled=True)]
    reduce_sum x6 -> x0, other arithmetic: 11.5 us -> none  [the longest x2 8.9 us: moe_layer(): jnp.sum(returned.reshape(EXPERTS, group_size, capacity, width).astype(jnp...]
    broadcast_in_dim x2 -> x0, local copies, waits for them, and re-layouts: 8.99 us -> none  [moe_layer(): outgoing = jnp.repeat(blocks, group_size, axis=0)]
    ppermute x2 -> x0, starting transfers between devices: 7.35 us -> none  [passed_along(): return lax.ppermute(value, axis, pairs)]
  transfers between devices with their start and end apart: 6 -> 0, of which waited for: 5 -> 0; matrix products, arithmetic and copies ran while one was open for 14% -> 0% of each run, Pallas kernels for 0% -> 0%
where the time goes in v1:
time: 171 us; the launch traced here: 168 us
  Pallas kernels  160 us (94%)
  local copies, waits for them, and re-layouts  7.2 us (4%)
    pallas_call x1, Pallas kernels, local(): pl.pallas_call(kernel, out_shape=(out, out), in_specs=[any_spec, any_spec...  160 us
    unnamed x12, local copies, waits for them, and re-layouts  7.2 us

profile of v1, /device:TPU:2, one launch (start us, length us, event | category | flops | bytes accessed | tf_op | source)
XLA Modules:
  0.0 168.1 jit_solution(3908213066887430566)
XLA Ops:
  0.6 0.7 add_bitcast_fusion.routes_ref
  1.4 0.0 copy-start
  1.4 1.5 copy-done
  2.9 0.0 copy-start.1
  2.9 1.2 copy-done.1
  4.1 0.0 copy-start.2
  4.1 1.2 copy-done.2
  5.2 0.0 copy-start.3
  5.2 0.7 copy-done.3
  6.0 0.0 copy-start.4
  6.0 0.7 copy-done.4
  6.7 159.5 %relay.1 = (bf16[64,7168]{1,0:T(8,128)(2,1)S(1)}, bf16[64,7168]{1,0:T(8,128)(2,1)S(1)}) custom-call(bf16[64,7168]{1,0:T(8,128)(2,1)S(1)} %bitcast.17, bf16[64,7168]{1,0:T(8,128)(2,1)S(1)} %bitcast.18, bf16[1,7168]{1,0:T(2,128)(2,1)S(1)} %copy-done.3, bf16[2,7168]{1,0:T(2,128)(2,1)S(1)} %bitcast.19, bf16[7168,128]{1,0:T(8,128)(2,1)S(1)} %bitcast.14, ...), custom_call_target="tpu_custom_call" | custom-call | tf_op jit(solution)/shard_map/relay/pallas_call | solution.py:423
  166.2 0.9 copy.13
  167.2 0.9 copy.14
Async XLA Ops:
  1.4 1.5 copy-start
  2.9 1.2 copy-start.1
  4.1 1.2 copy-start.2
  5.2 0.7 copy-start.3
  6.0 0.7 copy-start.4

commit v2 on v1

--- a/solution.py
+++ b/solution.py
@@ -28,10 +28,12 @@
 WD_Z, WD_RELAY, WD_CORE, WG_CORE, WU_CORE = range(W_BASE, W_BASE + 5)
 ACT_Z = W_BASE + 5
 R_BASE = ACT_Z + 4
-RET_XO, RET_XE, RET_ZO, RET_ZE, RET_C, RET_CF = range(R_BASE, R_BASE + 6 * NJ, NJ)
-OUT_UP = R_BASE + 6 * NJ
+RET_XO, RET_XE, RET_ZO, RET_ZC, RET_C = range(R_BASE, R_BASE + 5 * NJ, NJ)
+OUT_UP = R_BASE + 5 * NJ
 OUT_DN = OUT_UP + 2 * NJ
-N_SEM = OUT_DN + 2 * NJ
+RELAY_UP = OUT_DN + 2 * NJ
+RELAY_DN = RELAY_UP + NJ
+N_SEM = RELAY_DN + NJ
 
 
 def dot(a, b):
@@ -39,10 +41,10 @@
 
 
 def kernel(
-    up_ref, down_ref, gain_ref, router_ref, wg_ref, wu_ref, wd_ref, routes_ref,
+    up_ref, down_ref, gain_ref, router_ref, wg_ref, wu_ref, wd_ref, routes_up, routes_down,
     out_up, out_dn,
-    xin, xb, fb, wg, wu, wd, actm, actz, acc, sx, rx, sz, sc, rze, fa, fz, outb,
-    place, place_t, weight, local_sem, send_sem, recv_sem,
+    xin, gain_vm, router_vm, routes_vm, xb, fb, wg, wu, wd, actm, actz, acc, sx, rx, sz, sc, fa, fz, outb,
+    relay_up, relay_dn, place, place_t, weight, local_sem, send_sem, recv_sem,
 ):
     pp = lax.axis_index("pp")
     ep = lax.axis_index("ep")
@@ -57,10 +59,18 @@
     xn = device(xi + 1 - 2 * (xi % 2), zi, ci)
     zn = device(xi, 1 - zi, ci)
     xc = device(3 - xi, zi, ci)
+    xc_zn = device(3 - xi, 1 - zi, ci)
     core = device(xi, zi, 1 - ci)
     above = (lax.rem(pp + 1, n_pp), ep)
     below = (lax.rem(pp + n_pp - 1, n_pp), ep)
     expert = xi // 2
+
+    yi = pp % 4
+    low = yi == 0
+    high = yi == 3
+    across = (jnp.where(low, pp + 3, lax.rem(pp + n_pp - 3, n_pp)), ep)
+    next_row = (lax.rem(pp + 4, n_pp), ep)
+    last_row = (lax.rem(pp + n_pp - 4, n_pp), ep)
     my_half = zi * HALF
     other_half = (1 - zi) * HALF
 
@@ -125,14 +135,11 @@
     def ret_zo(j):
         return remote(sz.at[j, pl.ds(0, ROWS)], fz.at[j, pl.ds(0, ROWS)], RET_ZO + j, zn)
 
-    def ret_ze(j):
-        return remote(sz.at[j, pl.ds(ROWS, ROWS)], rze.at[j], RET_ZE + j, zn)
+    def ret_zc(j):
+        return remote(sz.at[j, pl.ds(ROWS, ROWS)], fz.at[j, pl.ds(ROWS, ROWS)], RET_ZC + j, xc_zn)
 
     def ret_c(j):
         return remote(sc.at[j], fa.at[j, pl.ds(ROWS, ROWS)], RET_C + j, xc)
-
-    def ret_cf(j):
-        return remote(rze.at[j], fz.at[j, pl.ds(ROWS, ROWS)], RET_CF + j, xc)
 
     def out_cols(j, part):
         start = (my_half if part == 0 else other_half) + j * JC
@@ -150,6 +157,32 @@
             outb.at[j, part, pl.ds(ROWS, ROWS)], out_dn.at[:, where], OUT_DN + 2 * j + part, below
         )
 
+    def detour_up(j):
+        return remote(outb.at[j, 0, pl.ds(0, ROWS)], relay_up.at[j], RELAY_UP + j, across)
+
+    def detour_dn(j):
+        return remote(outb.at[j, 0, pl.ds(ROWS, ROWS)], relay_dn.at[j], RELAY_DN + j, across)
+
+    def onward_up(j):
+        return pltpu.make_async_remote_copy(
+            src_ref=relay_up.at[j],
+            dst_ref=out_up.at[:, out_cols(j, 0)],
+            send_sem=send_sem.at[RELAY_UP + j],
+            recv_sem=recv_sem.at[OUT_UP + 2 * j],
+            device_id=next_row,
+            device_id_type=MESH,
+        )
+
+    def onward_dn(j):
+        return pltpu.make_async_remote_copy(
+            src_ref=relay_dn.at[j],
+            dst_ref=out_dn.at[:, out_cols(j, 0)],
+            send_sem=send_sem.at[RELAY_DN + j],
+            recv_sem=recv_sem.at[OUT_DN + 2 * j],
+            device_id=last_row,
+            device_id_type=MESH,
+        )
+
     def loop(count, body):
         def step(k, carry):
             body(k)
@@ -162,18 +195,36 @@
     load_wg = pltpu.make_async_copy(wg_ref, wg.at[0], local_sem.at[2])
     load_wu = pltpu.make_async_copy(wu_ref, wu.at[0], local_sem.at[3])
     load_wd = pltpu.make_async_copy(wd_ref.at[:, half_mine], wd.at[0], local_sem.at[4])
+    load_gain = pltpu.make_async_copy(gain_ref, gain_vm, local_sem.at[5])
+    load_router = pltpu.make_async_copy(router_ref, router_vm, local_sem.at[6])
+    load_ru = pltpu.make_async_copy(routes_up, routes_vm.at[0], local_sem.at[7])
+    load_rd = pltpu.make_async_copy(routes_down, routes_vm.at[1], local_sem.at[8])
     load_up.start()
     load_dn.start()
+    load_ru.start()
+    load_rd.start()
+    load_gain.start()
+    load_router.start()
     barrier = pltpu.get_barrier_semaphore()
     for to in (xn, zn, xc, core, above, below):
         pl.semaphore_signal(barrier, inc=1, device_id=to, device_id_type=MESH)
+
+    @pl.when(low | high)
+    def _():
+        for to in (across, next_row, last_row):
+            pl.semaphore_signal(barrier, inc=1, device_id=to, device_id_type=MESH)
+
     load_wg.start()
     load_wu.start()
     load_wd.start()
 
     token_r = lax.broadcasted_iota(jnp.int32, (128, 128), 0)
     token_c = lax.broadcasted_iota(jnp.int32, (128, 128), 1)
-    chosen = jnp.broadcast_to(routes_ref[...], (128, 128))
+    load_ru.wait()
+    load_rd.wait()
+    wide_up = dot(routes_vm[0].astype(F32), jnp.where(token_r[:64] == token_c[:64], 1.0, 0.0))
+    wide_dn = dot(routes_vm[1].astype(F32), jnp.where(token_r[:64] + 64 == token_c[:64], 1.0, 0.0))
+    chosen = jnp.broadcast_to((wide_up + wide_dn).astype(jnp.int32), (128, 128))
     mine = (chosen == expert).astype(F32)
     before = ((token_r < token_c) & (token_r // 64 == token_c // 64)).astype(F32)
     ahead = dot(mine.astype(BF16), before.astype(BF16))
@@ -196,10 +247,12 @@
     weight[...] = jnp.broadcast_to(inverse, (128, 128))
 
     def normed(k):
-        gain = gain_ref[:, cols(k)].astype(F32)
+        gain = gain_vm[:, cols(k)].astype(F32)
         return (xin[:, cols(k)].astype(F32) * weight[:, 0:1] * gain).astype(BF16)
 
-    pl.semaphore_wait(barrier, 6)
+    load_gain.wait()
+    load_router.wait()
+    pl.semaphore_wait(barrier, jnp.where(low | high, 9, 6))
 
     def first(k):
         moved = dot(place[...], normed(k)).astype(BF16)
@@ -217,7 +270,7 @@
     def affinity(k, carry):
         zero, one = carry
         part = normed(k).astype(F32)
-        near = router_ref[:, cols(k)].astype(F32)
+        near = router_vm[:, cols(k)].astype(F32)
         zero = zero + jnp.sum(part * near[0:1], axis=1, keepdims=True)
         one = one + jnp.sum(part * near[1:2], axis=1, keepdims=True)
         return zero, one
@@ -362,26 +415,51 @@
         ret_xe(j).wait_recv()
         far = far + rx[j, 128:256].astype(F32)
         sz[j, ROWS:128] = far[ROWS:].astype(BF16)
-        ret_ze(j).start()
+        ret_zc(j).start()
         sc[j] = far[:ROWS].astype(BF16)
         ret_c(j).start()
-
-    def onward(j):
-        ret_ze(j).wait_recv()
-        ret_cf(j).start()
 
     def finish(j, part, held):
         mixed = dot(place_t[...], held[j])
         out = xin[:, out_cols(j, part)].astype(F32) + weight[:, 0:1] * mixed
         outb[j, part] = out.astype(BF16)
-        send_up(j, part).start()
-        send_dn(j, part).start()
+        if part == 1:
+            send_up(j, 1).start()
+            send_dn(j, 1).start()
+            return
+
+        @pl.when(high)
+        def _():
+            detour_up(j).start()
+
+        @pl.when(~high)
+        def _():
+            send_up(j, 0).start()
+
+        @pl.when(low)
+        def _():
+            detour_dn(j).start()
+
+        @pl.when(~low)
+        def _():
+            send_dn(j, 0).start()
+
+    def onward(j):
+        @pl.when(low)
+        def _():
+            detour_up(j).wait_recv()
+            onward_up(j).start()
+
+        @pl.when(high)
+        def _():
+            detour_dn(j).wait_recv()
+            onward_dn(j).start()
 
     def final(j):
         ret_c(j).wait_recv()
         finish(j, 0, fa)
         ret_zo(j).wait_recv()
-        ret_cf(j).wait_recv()
+        ret_zc(j).wait_recv()
         finish(j, 1, fz)
 
     def tail(i):
@@ -389,26 +467,44 @@
         def _():
             sums(i)
 
-        @pl.when((i >= 1) & (i < NJ + 1))
-        def _():
-            onward(i - 1)
-
-        @pl.when(i >= 2)
+        @pl.when((i >= 2) & (i < NJ + 2))
         def _():
             final(i - 2)
 
-    loop(NJ + 2, tail)
+        @pl.when(i >= 3)
+        def _():
+            onward(i - 3)
+
+    loop(NJ + 3, tail)
 
     def last(j):
         ret_xo(j).wait_send()
         ret_xe(j).wait_send()
         ret_zo(j).wait_send()
-        ret_ze(j).wait_send()
+        ret_zc(j).wait_send()
         ret_c(j).wait_send()
-        ret_cf(j).wait_send()
+        send_up(j, 1).wait_send()
+        send_dn(j, 1).wait_send()
+
+        @pl.when(high)
+        def _():
+            detour_up(j).wait_send()
+            onward_dn(j).wait_send()
+
+        @pl.when(~high)
+        def _():
+            send_up(j, 0).wait_send()
+
+        @pl.when(low)
+        def _():
+            detour_dn(j).wait_send()
+            onward_up(j).wait_send()
+
+        @pl.when(~low)
+        def _():
+            send_dn(j, 0).wait_send()
+
         for part in range(2):
-            send_up(j, part).wait_send()
-            send_dn(j, part).wait_send()
             send_up(j, part).wait_recv()
             send_dn(j, part).wait_recv()
 
@@ -416,17 +512,18 @@
 
 
 def local(stream_up, stream_down, norm_gain, router, w_gate, w_up, w_down, routes_up, routes_down):
-    routes = jnp.concatenate([routes_up[0, 0, :, 0], routes_down[0, 0, :, 0]])[None]
     any_spec = pl.BlockSpec(memory_space=pl.ANY)
-    vmem_spec = pl.BlockSpec(memory_space=pltpu.VMEM)
     out = jax.ShapeDtypeStruct((ROWS, D), BF16)
     rising, falling = pl.pallas_call(
         kernel,
         out_shape=(out, out),
-        in_specs=[any_spec, any_spec, vmem_spec, vmem_spec, any_spec, any_spec, any_spec, vmem_spec],
+        in_specs=[any_spec] * 9,
         out_specs=(any_spec, any_spec),
         scratch_shapes=[
             pltpu.VMEM((128, D), BF16),
+            pltpu.VMEM((1, D), BF16),
+            pltpu.VMEM((2, D), BF16),
+            pltpu.VMEM((2, 1, ROWS), jnp.int32),
             pltpu.VMEM((8, ROWS, D), BF16),
             pltpu.VMEM((ROWS, D), BF16),
             pltpu.VMEM((2, D, HID), BF16),
@@ -439,23 +536,25 @@
             pltpu.VMEM((NJ, 4 * ROWS, JC), BF16),
             pltpu.VMEM((NJ, 2 * ROWS, JC), BF16),
             pltpu.VMEM((NJ, ROWS, JC), BF16),
-            pltpu.VMEM((NJ, ROWS, JC), BF16),
             pltpu.VMEM((NJ, 2 * ROWS, JC), BF16),
             pltpu.VMEM((NJ, 2 * ROWS, JC), BF16),
             pltpu.VMEM((NJ, 2, 2 * ROWS, JC), BF16),
+            pltpu.VMEM((NJ, ROWS, JC), BF16),
+            pltpu.VMEM((NJ, ROWS, JC), BF16),
             pltpu.VMEM((128, 128), BF16),
             pltpu.VMEM((128, 128), BF16),
             pltpu.VMEM((128, 128), F32),
-            pltpu.SemaphoreType.DMA((5,)),
+            pltpu.SemaphoreType.DMA((9,)),
             pltpu.SemaphoreType.DMA((N_SEM,)),
             pltpu.SemaphoreType.DMA((N_SEM,)),
         ],
         compiler_params=pltpu.CompilerParams(
-            collective_id=0, has_side_effects=True, vmem_limit_bytes=48 * 2**20
+            collective_id=0, has_side_effects=True, vmem_limit_bytes=60 * 2**20
         ),
         name="relay",
     )(
-        stream_up[0], stream_down[0], norm_gain, router[0].T, w_gate[0], w_up[0], w_down[0], routes
+        stream_up[0], stream_down[0], norm_gain, router[0].T, w_gate[0], w_up[0], w_down[0],
+        routes_up.reshape(1, ROWS), routes_down.reshape(1, ROWS),
     )
     return rising[None], falling[None]
 

time: 171 us -> 147 us (0.86); the launches traced: 168 us -> 146 us
  Pallas kernels: 160 us -> 142 us
  local copies, waits for them, and re-layouts: 7.2 us -> 3.17 us
    pallas_call x1, Pallas kernels: 160 us -> 142 us  [local(): pl.pallas_call(kernel, out_shape=(out, out), in_specs=[any_spec] * 9, out...]
    unnamed x12 -> x4, local copies, waits for them, and re-layouts: 7.2 us -> 3.17 us
where the time goes in v2:
time: 147 us; the launch traced here: 146 us
  Pallas kernels  142 us (97%)
  local copies, waits for them, and re-layouts  3.17 us (2%)
    pallas_call x1, Pallas kernels, local(): pl.pallas_call(kernel, out_shape=(out, out), in_specs=[any_spec] * 9, out...  142 us
    unnamed x4, local copies, waits for them, and re-layouts  3.17 us

profile of v2, /device:TPU:2, one launch (start us, length us, event | category | flops | bytes accessed | tf_op | source)
XLA Modules:
  0.0 146.3 jit_solution(4047413507499338194)
XLA Ops:
  0.6 142.5 %relay.1 = (bf16[64,7168]{1,0:T(8,128)(2,1)}, bf16[64,7168]{1,0:T(8,128)(2,1)}) custom-call(bf16[64,7168]{1,0:T(8,128)(2,1)} %bitcast.15, bf16[64,7168]{1,0:T(8,128)(2,1)} %bitcast.16, bf16[1,7168]{1,0:T(2,128)(2,1)} %gain_ref.1, bf16[2,7168]{1,0:T(2,128)(2,1)} %bitcast.19, bf16[7168,128]{1,0:T(8,128)(2,1)} %bitcast.12, bf16[7168,128]{1,0:T(8,128)(2,1)} %bitcast.13, ...), custom_call_target="tpu_custom_call" | custom-call | tf_op jit(solution)/shard_map/relay/pallas_call | solution.py:517
  143.1 0.0 copy-start
  143.1 2.2 %copy.13 = bf16[1,64,7168]{2,1,0:T(8,128)(2,1)} copy(bf16[1,64,7168]{2,1,0:T(8,128)(2,1)} %bitcast.18) | data formatting | bytes 1835008
  145.4 0.0 copy-done
  145.4 0.9 copy.14
Async XLA Ops:
  143.1 2.3 %copy-start = (bf16[64,7168]{1,0:T(8,128)(2,1)S(1)}, bf16[64,7168]{1,0:T(8,128)(2,1)}, u32[]{:S(2)}) copy-start(bf16[64,7168]{1,0:T(8,128)(2,1)} %get-tuple-element.5) | copy-start | bytes 2752516

commit v3 on v1

v3 whole, which is shorter than its diff:
```python
import jax
import jax.numpy as jnp
from jax import lax
from jax.experimental import pallas as pl
from jax.experimental.pallas import tpu as pltpu
from jax.sharding import PartitionSpec as P

MESH = pl.DeviceIdType.MESH
F32 = jnp.float32
BF16 = jnp.bfloat16
EPSILON = 1e-06
ROUTE_SCALE = 2.5

D = 7168
ROWS = 64
HID = 128
HALF = D // 2
KC = 1024
NK = D // KC
JC = 512
NJ = HALF // JC
NB = NJ - 2
NR = NB + 4
KX = 3

OWN, Z_OWN, ENT, Z_ENT, X_OWN, D_OWN, X_ENT, D_ENT = range(8)

OWN_X, OWN_Z, CROSS, ENT_X, ENT_Z, FWD_OWN, FWD_ENT = range(0, 7 * NK, NK)
W_BASE = 7 * NK
WD_Z, WD_RELAY, WD_CORE, WG_CORE, WU_CORE = range(W_BASE, W_BASE + 5)
ACT_Z = W_BASE + 5
R_BASE = ACT_Z + 4
RET_XO, RET_XE, RET_ZO, RET_ZC, RET_C = range(R_BASE, R_BASE + 5 * NR, NR)
OUT_UP = R_BASE + 5 * NR
OUT_DN = OUT_UP + 4 * NJ
RELAY = OUT_DN + 4 * NJ
ONWARD = RELAY + 4 * NJ
PERM_UP = ONWARD + 4 * NJ
PERM_DN = PERM_UP + 1
N_SEM = PERM_DN + 1


def dot(a, b):
    return jnp.dot(a, b, preferred_element_type=F32)


def kernel(
    up_ref, down_ref, gain_ref, router_ref, wg_ref, wu_ref, wd_ref, routes_up, routes_down,
    out_up, out_dn, out_perm,
    xin, xs, gain_vm, router_vm, routes_vm, xb, fb, wg, wu, wd, actm, actz, acc, sx, rx, sz, sc, fc, fz, outb,
    via, place, perm, weight, local_sem, send_sem, recv_sem, ready,
):
    pp = lax.axis_index("pp")
    ep = lax.axis_index("ep")
    n_pp = lax.axis_size("pp")
    xi = ep // 4
    zi = (ep // 2) % 2
    ci = ep % 2

    def device(x, z, c):
        return (pp, x * 4 + z * 2 + c)

    xn = device(xi + 1 - 2 * (xi % 2), zi, ci)
    zn = device(xi, 1 - zi, ci)
    xc = device(3 - xi, zi, ci)
    xc_zn = device(3 - xi, 1 - zi, ci)
    core = device(xi, zi, 1 - ci)
    above = (lax.rem(pp + 1, n_pp), ep)
    below = (lax.rem(pp + n_pp - 1, n_pp), ep)
    expert = xi // 2

    yi = pp % 4
    falls = yi == 0

    def section(step):
        return (lax.rem(pp + n_pp + step, n_pp), ep)

    my_half = zi * HALF
    other_half = (1 - zi) * HALF

    def remote(src, dst, index, to):
        return pltpu.make_async_remote_copy(
            src_ref=src,
            dst_ref=dst,
            send_sem=send_sem.at[index],
            recv_sem=recv_sem.at[index],
            device_id=to,
            device_id_type=MESH,
        )

    def cols(k):
        return pl.ds(pl.multiple_of(k * KC, KC), KC)

    def block(slot, k):
        return xb.at[slot, :, cols(k)]

    def own_x(k):
        return remote(block(OWN, k), block(X_OWN, k), OWN_X + k, xn)

    def own_z(k):
        return remote(block(OWN, k), block(Z_OWN, k), OWN_Z + k, zn)

    def cross(k):
        return remote(fb.at[:, cols(k)], block(ENT, k), CROSS + k, xc)

    def ent_x(k):
        return remote(block(ENT, k), block(X_ENT, k), ENT_X + k, xn)

    def ent_z(k):
        return remote(block(ENT, k), block(Z_ENT, k), ENT_Z + k, zn)

    def fwd_own(k):
        return remote(block(Z_OWN, k), block(D_OWN, k), FWD_OWN + k, xn)

    def fwd_ent_x(k):
        return remote(block(Z_ENT, k), block(D_ENT, k), FWD_ENT + k, xn)

    def fwd_ent_z(k):
        return remote(block(X_ENT, k), block(D_ENT, k), FWD_ENT + k, zn)

    half_mine = pl.ds(pl.multiple_of(my_half, HALF), HALF)
    half_other = pl.ds(pl.multiple_of(other_half, HALF), HALF)
    wd_z = remote(wd_ref.at[:, half_other], wd.at[2], WD_Z, zn)
    wd_relay = remote(wd.at[2], wd.at[3], WD_RELAY, core)
    wd_core = remote(wd_ref.at[:, half_mine], wd.at[1], WD_CORE, core)
    wg_core = remote(wg_ref, wg.at[1], WG_CORE, core)
    wu_core = remote(wu_ref, wu.at[1], WU_CORE, core)

    def act_z(pair):
        rows = pl.ds(pair * 2 * ROWS, 2 * ROWS)
        return remote(actm.at[rows], actz.at[rows], ACT_Z + pair, zn)

    def piece(j, streams=(0, 1)):
        p = j + 2 if streams == (1,) else j
        return p, j, pl.multiple_of(j * JC, JC), streams

    def span(streams, base, rows):
        return pl.ds(base + streams[0] * rows, len(streams) * rows)

    def ret_xo(p, j, at, streams):
        part = (span(streams, 0, ROWS), pl.ds(at, JC))
        return remote(sx.at[part], rx.at[part], RET_XO + p, xn)

    def ret_xe(p, j, at, streams):
        part = (span(streams, 128, ROWS), pl.ds(at, JC))
        return remote(sx.at[part], rx.at[part], RET_XE + p, xn)

    def ret_zo(p, j, at, streams):
        part = (span(streams, 0, 32), pl.ds(at, JC))
        return remote(sz.at[part], fz.at[part], RET_ZO + p, zn)

    def ret_zc(p, j, at, streams):
        part = (span(streams, ROWS, 32), pl.ds(at, JC))
        return remote(sz.at[part], fz.at[part], RET_ZC + p, xc_zn)

    def ret_c(p, j, at, streams):
        part = (span(streams, 0, 32), pl.ds(at, JC))
        return remote(sc.at[part], fc.at[part], RET_C + p, xc)

    def out_cols(at, n, half):
        start = jnp.where(half == 0, my_half, other_half) + at
        return pl.ds(pl.multiple_of(start, 128), n)

    def moved(src, dst, send, recv, to):
        return pltpu.make_async_remote_copy(
            src_ref=src,
            dst_ref=dst,
            send_sem=send_sem.at[send],
            recv_sem=recv_sem.at[recv],
            device_id=to,
            device_id_type=MESH,
        )

    def out_src(q, stream, at):
        return outb.at[q % 2, pl.ds(q // 2 * ROWS + stream * 32, 32), pl.ds(at, JC)]

    def row_at(q):
        row = q // 2 * 32
        return pl.ds(row if isinstance(q, int) else pl.multiple_of(row, 32), 32)

    def out_dst(ref, q, at):
        return ref.at[row_at(q), out_cols(at, JC, q % 2)]

    def send_up(stream, j, at, q):
        index = OUT_UP + 4 * j + q
        return moved(out_src(q, stream, at), out_dst(out_up, q, at), index, index, above)

    def send_dn(stream, j, at, q):
        index = OUT_DN + 4 * j + q
        return moved(out_src(q, stream, at), out_dst(out_dn, q, at), index, index, below)

    def turn(j, q):
        return jnp.where((j >= NB) & (q >= 2), 3, lax.rem(j + q, 4))

    def via_at(q, at):
        return via.at[q % 2, row_at(q), pl.ds(at, JC)]

    def detour(j, at, q):
        index = RELAY + 4 * j + q
        step = 3 - turn(j, q)
        to = section(jnp.where(falls, step, -step))
        return moved(out_src(q, 0, at), via_at(q, at), index, index, to)

    def arrived(j, at, q):
        index = RELAY + 4 * j + q
        return moved(via_at(q, at), via_at(q, at), index, index, above)

    def onward_up(j, at, q):
        dst = out_dst(out_up, q, at)
        index = 4 * j + q
        return moved(via_at(q, at), dst, ONWARD + index, OUT_UP + index, section(4 - yi))

    def onward_dn(j, at, q):
        dst = out_dst(out_dn, q, at)
        index = 4 * j + q
        return moved(via_at(q, at), dst, ONWARD + index, OUT_DN + index, section(-1 - yi))

    def perm_up(stream):
        return moved(perm.at[stream], out_perm.at[0], PERM_UP, PERM_UP, above)

    def perm_dn(stream):
        return moved(perm.at[stream], out_perm.at[1], PERM_DN, PERM_DN, below)

    def by_stream(act_0, act_1):
        @pl.when(falls)
        def _():
            act_0(1)
            act_1(0)

        @pl.when(~falls)
        def _():
            act_0(0)
            act_1(1)

    def loop(count, body):
        def step(k, carry):
            body(k)
            return carry

        lax.fori_loop(0, count, step, 0)

    def load_x(s, src):
        return pltpu.make_async_copy(src, xin.at[pl.ds(s * ROWS, ROWS)], local_sem.at[s])

    def load_routes(s, src):
        return pltpu.make_async_copy(src, routes_vm.at[s], local_sem.at[7 + s])

    def load_streams(first, second, routes_first, routes_second):
        load_x(0, first).start()
        load_x(1, second).start()
        load_routes(0, routes_first).start()
        load_routes(1, routes_second).start()

    @pl.when(falls)
    def _():
        load_streams(down_ref, up_ref, routes_down, routes_up)

    @pl.when(~falls)
    def _():
        load_streams(up_ref, down_ref, routes_up, routes_down)

    load_wg = pltpu.make_async_copy(wg_ref, wg.at[0], local_sem.at[2])
    load_wu = pltpu.make_async_copy(wu_ref, wu.at[0], local_sem.at[3])
    load_wd = pltpu.make_async_copy(wd_ref.at[:, half_mine], wd.at[0], local_sem.at[4])
    load_gain = pltpu.make_async_copy(gain_ref, gain_vm, local_sem.at[5])
    load_router = pltpu.make_async_copy(router_ref, router_vm, local_sem.at[6])
    load_gain.start()
    load_router.start()
    barrier = pltpu.get_barrier_semaphore()
    near = (xn, zn, xc, xc_zn, core)
    steps = (-4, -3, -2, -1, 1, 2, 3, 4)
    lower = sum((section(step)[0] < pp).astype(jnp.int32) for step in steps)
    for to in near:
        pl.semaphore_signal(barrier, inc=1, device_id=to, device_id_type=MESH)
    for step in steps:
        to = section(step)

        @pl.when(to[0] > pp)
        def _():
            pl.semaphore_signal(barrier, inc=1, device_id=to, device_id_type=MESH)

    load_wg.start()
    load_wu.start()
    load_wd.start()

    token_r = lax.broadcasted_iota(jnp.int32, (128, 128), 0)
    token_c = lax.broadcasted_iota(jnp.int32, (128, 128), 1)
    load_routes(0, routes_up).wait()
    load_routes(1, routes_down).wait()
    wide_0 = dot(routes_vm[0].astype(F32), jnp.where(token_r[:64] == token_c[:64], 1.0, 0.0))
    wide_1 = dot(routes_vm[1].astype(F32), jnp.where(token_r[:64] + 64 == token_c[:64], 1.0, 0.0))
    chosen = jnp.broadcast_to((wide_0 + wide_1).astype(jnp.int32), (128, 128))
    mine = (chosen == expert).astype(F32)
    before = ((token_r < token_c) & (token_r // 64 == token_c // 64)).astype(F32)
    ahead = dot(mine.astype(BF16), before.astype(BF16))
    inside = (token_c % 64).astype(F32)
    stream = (token_c // 64 * 32).astype(F32)
    target = stream + jnp.where(mine > 0.5, ahead, 64.0 + inside - ahead)
    hit = (token_r.astype(F32) == target).astype(F32)
    place[...] = hit.astype(BF16)
    back_to = stream * 2.0 + jnp.where(mine > 0.5, ahead, 32.0 + inside - ahead)
    back_hit = (token_r.astype(F32) == back_to).astype(F32).T.astype(BF16)
    perm[...] = jnp.zeros_like(perm)
    perm[0, :, 0:ROWS] = back_hit[:ROWS, :ROWS]
    perm[1, :, 0:ROWS] = back_hit[ROWS:, ROWS:]

    load_x(0, up_ref).wait()
    load_x(1, down_ref).wait()

    def squares(k, total):
        part = xin[:, cols(k)].astype(F32)
        part = part * part
        for c in range(KC // 128):
            total = total + part[:, c * 128:(c + 1) * 128]
        return total

    total = lax.fori_loop(0, NK, squares, jnp.zeros((128, 128), F32))
    total = jnp.sum(total, axis=1, keepdims=True)
    inverse = lax.rsqrt(total * (1.0 / D) + EPSILON)
    weight[...] = jnp.broadcast_to(inverse, (128, 128))

    def normed(k):
        gain = gain_vm[:, cols(k)].astype(F32)
        return (xin[:, cols(k)].astype(F32) * weight[:, 0:1] * gain).astype(BF16)

    load_gain.wait()
    load_router.wait()
    pl.semaphore_wait(barrier, len(near) + lower)
    for step in steps:
        to = section(step)

        @pl.when(to[0] < pp)
        def _():
            pl.semaphore_signal(ready, inc=1, device_id=to, device_id_type=MESH)


    def first(k):
        moved = dot(place[...], normed(k)).astype(BF16)
        xb[OWN, :, cols(k)] = moved[:ROWS]
        fb[:, cols(k)] = moved[ROWS:]
        cross(k).start()
        own_x(k).start()
        own_z(k).start()

    loop(NK, first)
    wg_core.start()
    wu_core.start()
    wd_core.start()

    def affinity(k, carry):
        own, foreign = carry
        zero = router_vm[0:1, cols(k)].astype(F32)
        one = router_vm[1:2, cols(k)].astype(F32)
        near, far = jnp.where(expert == 0, zero, one), jnp.where(expert == 0, one, zero)
        own = own + jnp.sum(xb[OWN, :, cols(k)].astype(F32) * near, axis=1, keepdims=True)
        foreign = foreign + jnp.sum(fb[:, cols(k)].astype(F32) * far, axis=1, keepdims=True)
        xs[:, cols(k)] = dot(place[...], xin[:, cols(k)]).astype(BF16)
        return own, foreign

    empty = jnp.zeros((ROWS, 1), F32)
    own, foreign = lax.fori_loop(0, NK, affinity, (empty, empty))
    weight[0:ROWS] = jnp.broadcast_to(ROUTE_SCALE * jax.nn.sigmoid(own), (ROWS, 128))
    weight[ROWS:] = jnp.broadcast_to(ROUTE_SCALE * jax.nn.sigmoid(foreign), (ROWS, 128))

    load_wg.wait()
    load_wu.wait()
    load_wd.wait()
    wg_core.wait_recv()
    wu_core.wait_recv()

    def hidden_step(pair, k):
        rows = xb[pl.ds(2 * pair, 2), :, cols(k)].reshape(2 * ROWS, KC)
        gate = dot(rows, jnp.concatenate([wg[0, cols(k)], wg[1, cols(k)]], axis=1))
        up = dot(rows, jnp.concatenate([wu[0, cols(k)], wu[1, cols(k)]], axis=1))
        first_one = k == 0
        acc[:, 0:256] = jnp.where(first_one, 0.0, acc[:, 0:256]) + gate
        acc[:, 256:512] = jnp.where(first_one, 0.0, acc[:, 256:512]) + up

    def hidden_end(pair):
        act = jax.nn.silu(acc[:, 0:256]) * acc[:, 256:512]
        act = act.astype(BF16)
        for n, row in enumerate((0, ROWS, 32, ROWS + 32)):
            actm[pl.ds(pair * 2 * ROWS + n * 32, 32)] = act[row:row + 32]
        act_z(pair).start()

    acc[...] = jnp.zeros_like(acc)

    def second(k):
        cross(k).wait_recv()
        ent_x(k).start()
        ent_z(k).start()
        own_z(k).wait_recv()
        fwd_own(k).start()
        hidden_step(0, k)

    loop(NK, second)
    wd_z.start()

    @pl.when(lower < len(steps))
    def _():
        pl.semaphore_wait(ready, len(steps) - lower)

    by_stream(lambda s: perm_up(s).start(), lambda s: perm_dn(s).start())
    hidden_end(0)

    def third(k):
        ent_z(k).wait_recv()

        @pl.when(k < KX)
        def _():
            fwd_ent_x(k).start()

        hidden_step(1, k)

    loop(NK, third)
    hidden_end(1)

    def fourth(k):
        own_x(k).wait_recv()
        fwd_own(k).wait_recv()
        hidden_step(2, k)

    loop(NK, fourth)
    hidden_end(2)

    def relay(k):
        ent_x(k).wait_recv()

        @pl.when(k >= KX)
        def _():
            fwd_ent_z(k).start()

    loop(NK, relay)
    wd_z.wait_recv()
    wd_relay.start()
    wd_core.wait_recv()

    def back(pair, at, streams):
        base = pair * 2 * ROWS
        far = []
        for s in streams:
            first = base + s * ROWS
            far += [actz[first + 32:first + 64], actz[first:first + 32]]
        first = base + streams[0] * ROWS
        near = actm[first:first + len(streams) * ROWS]
        left = jnp.concatenate([near, jnp.concatenate(far, axis=0)], axis=1)
        return dot(left, wd[:, :, pl.ds(at, JC)].reshape(4 * HID, JC))

    def back_o(p, j, at, streams):
        sx[span(streams, 0, ROWS), pl.ds(at, JC)] = back(2, at, streams).astype(BF16)
        ret_xo(p, j, at, streams).start()

    def back_e(p, j, at, streams):
        sx[span(streams, 128, ROWS), pl.ds(at, JC)] = back(3, at, streams).astype(BF16)
        ret_xe(p, j, at, streams).start()

    def finish(j, at, q, total, streams):
        rows = span(streams, q // 2 * ROWS, 32)
        out = xs[rows, out_cols(at, JC, q % 2)].astype(F32) + weight[rows, 0:1] * total
        outb[q % 2, rows, pl.ds(at, JC)] = out.astype(BF16)
        if 0 in streams:
            straight = (turn(j, q) == 3) | (yi == 1) | (yi == 2)

            @pl.when(straight & falls)
            def _():
                send_dn(0, j, at, q).start()

            @pl.when(straight & ~falls)
            def _():
                send_up(0, j, at, q).start()

            @pl.when(~straight)
            def _():
                detour(j, at, q).start()

        if 1 in streams:

            @pl.when(falls)
            def _():
                send_up(1, j, at, q).start()

            @pl.when(~falls)
            def _():
                send_dn(1, j, at, q).start()

    def parted(total):
        blocks = [[total[r:r + 32] for r in range(b, total.shape[0], ROWS)] for b in (0, 32)]
        return [jnp.concatenate(b, axis=0) for b in blocks]

    def sums_o(p, j, at, streams):
        total = back(0, at, streams)
        ret_xo(p, j, at, streams).wait_recv()
        total = total + rx[span(streams, 0, ROWS), pl.ds(at, JC)].astype(F32)
        mine_o, other = parted(total)
        sz[span(streams, 0, 32), pl.ds(at, JC)] = other.astype(BF16)
        ret_zo(p, j, at, streams).start()
        finish(j, at, 0, mine_o, streams)

    def sums_e(p, j, at, streams):
        total = back(1, at, streams)
        ret_xe(p, j, at, streams).wait_recv()
        total = total + rx[span(streams, 128, ROWS), pl.ds(at, JC)].astype(F32)
        mine_e, other = parted(total)
        sz[span(streams, ROWS, 32), pl.ds(at, JC)] = other.astype(BF16)
        ret_zc(p, j, at, streams).start()
        sc[span(streams, 0, 32), pl.ds(at, JC)] = mine_e.astype(BF16)
        ret_c(p, j, at, streams).start()

    def final_o(p, j, at, streams):
        ret_zo(p, j, at, streams).wait_recv()
        finish(j, at, 1, fz[span(streams, 0, 32), pl.ds(at, JC)].astype(F32), streams)

    def final_e(p, j, at, streams):
        ret_c(p, j, at, streams).wait_recv()
        finish(j, at, 2, fc[span(streams, 0, 32), pl.ds(at, JC)].astype(F32), streams)
        ret_zc(p, j, at, streams).wait_recv()
        finish(j, at, 3, fz[span(streams, ROWS, 32), pl.ds(at, JC)].astype(F32), streams)

    def relays(j):
        return lax.rem(yi + 4 * NJ - j, 4), lax.rem(3 - yi + 4 * NJ - j, 4)

    def pass_on(kind, p, j, at, streams):
        up, dn = relays(j)

        @pl.when((yi != 3) & (up // 2 == kind))
        def _():
            arrived(j, at, up).wait_recv()
            onward_up(j, at, up).start()

        @pl.when((yi != 0) & (dn // 2 == kind))
        def _():
            arrived(j, at, dn).wait_recv()
            onward_dn(j, at, dn).start()

    def fifth(k):
        fwd_ent_x(k).wait_recv()
        hidden_step(3, k)

    act_z(2).wait_recv()
    wd_relay.wait_recv()
    loop(2, lambda j: back_o(*piece(j)))
    loop(KX, fifth)
    loop(NB - 2, lambda j: back_o(*piece(j + 2)))
    act_z(0).wait_recv()
    act_z(1).wait_recv()

    def sixth(k):
        fwd_ent_z(k + KX).wait_recv()
        hidden_step(3, k + KX)

    loop(NK - KX - 1, sixth)
    sums_o(*piece(0))
    sixth(NK - KX - 1)
    hidden_end(3)
    sums_o(*piece(1))
    sums_o(*piece(2))

    def drain(k):
        own_x(k).wait_send()
        own_z(k).wait_send()
        cross(k).wait_send()
        ent_x(k).wait_send()
        ent_z(k).wait_send()
        fwd_own(k).wait_send()
        fwd_ent_x(k).wait_send()

    loop(NK, drain)
    act_z(3).wait_recv()
    first = [piece(NB, (0,)), piece(NB + 1, (0,))]
    second = [piece(NB, (1,)), piece(NB + 1, (1,))]
    loop(2, lambda j: back_e(*piece(j)))
    for part in first:
        back_o(*part)

    def step(i):
        @pl.when(i + 2 < NB)
        def _():
            back_e(*piece(i + 2))

        @pl.when(i == NB - 3)
        def _():
            for part in first:
                back_e(*part)

        @pl.when(i == NB - 2)
        def _():
            for part in second:
                back_e(*part)
            for part in second:
                back_o(*part)
            for part in first:
                sums_o(*part)

        @pl.when(i + 3 < NB)
        def _():
            sums_o(*piece(i + 3))

        final_o(*piece(i))
        sums_e(*piece(i))

        @pl.when(i >= 1)
        def _():
            final_e(*piece(i - 1))

        @pl.when(i >= 2)
        def _():
            pass_on(0, *piece(i - 2))

        @pl.when(i >= 3)
        def _():
            pass_on(1, *piece(i - 3))

    loop(NB, step)
    for part in first:
        final_o(*part)
    sums_e(*first[0])
    final_e(*piece(NB - 1))
    sums_e(*first[1])
    pass_on(0, *piece(NB - 2))
    pass_on(0, *piece(NB - 1))
    pass_on(1, *piece(NB - 3))
    pass_on(1, *piece(NB - 2))
    pass_on(0, *first[0])
    pass_on(0, *first[1])
    sums_e(*second[0])
    final_e(*first[0])
    sums_e(*second[1])
    final_e(*first[1])
    pass_on(1, *piece(NB - 1))
    sums_o(*second[0])
    sums_o(*second[1])
    final_e(*second[0])
    final_o(*second[0])
    final_e(*second[1])
    final_o(*second[1])

    for copy in (wd_z, wd_relay, wd_core, wg_core, wu_core, act_z(0), act_z(1), act_z(2), act_z(3)):
        copy.wait_send()
    by_stream(lambda s: perm_up(s).wait(), lambda s: perm_dn(s).wait())

    def sent(p, j, at, streams):
        ret_xo(p, j, at, streams).wait_send()
        ret_xe(p, j, at, streams).wait_send()
        ret_zo(p, j, at, streams).wait_send()
        ret_zc(p, j, at, streams).wait_send()
        ret_c(p, j, at, streams).wait_send()

    def last(p, j, at, streams):
        up, dn = relays(j)

        @pl.when((yi != 3) & ((j < NB) | (up < 2)))
        def _():
            onward_up(j, at, up).wait_send()

        @pl.when((yi != 0) & ((j < NB) | (dn < 2)))
        def _():
            onward_dn(j, at, dn).wait_send()

        for q in range(4):
            straight = (turn(j, q) == 3) | (yi == 1) | (yi == 2)

            @pl.when(falls)
            def _():
                send_up(1, j, at, q).wait_send()

            @pl.when(~falls)
            def _():
                send_dn(1, j, at, q).wait_send()

            @pl.when(straight & falls)
            def _():
                send_dn(0, j, at, q).wait_send()

            @pl.when(straight & ~falls)
            def _():
                send_up(0, j, at, q).wait_send()

            @pl.when(~straight)
            def _():
                detour(j, at, q).wait_send()

            send_up(0, j, at, q).wait_recv()
            send_dn(0, j, at, q).wait_recv()

    loop(NB, lambda j: sent(*piece(j)))
    for part in first + second:
        sent(*part)
    loop(NJ, lambda j: last(*piece(j)))


def reorder(up_ref, down_ref, perm_ref, out_up, out_down, perm, rows, outs, sem):
    load_perm = pltpu.make_async_copy(perm_ref, perm, sem.at[0])
    load_perm.start()
    loads, stores = [], []
    for k in range(0, D, KC):
        cols = pl.ds(k, KC)
        for stream, (src, dst) in enumerate(((up_ref, out_up), (down_ref, out_down))):
            n = len(loads)
            held = rows.at[stream, :, cols]
            loads.append(pltpu.make_async_copy(src.at[:, cols], held, sem.at[1 + n]))
            done = outs.at[stream, :, cols]
            stores.append(pltpu.make_async_copy(done, dst.at[:, cols], sem.at[1 + 2 * NK + n]))
    for load in loads:
        load.start()
    load_perm.wait()
    for n, (load, store) in enumerate(zip(loads, stores)):
        stream, cols = n % 2, pl.ds(n // 2 * KC, KC)
        load.wait()
        outs[stream, :, cols] = dot(perm[stream, :, 0:ROWS], rows[stream, :, cols]).astype(BF16)
        store.start()
    for store in stores:
        store.wait()


def local(stream_up, stream_down, norm_gain, router, w_gate, w_up, w_down, routes_up, routes_down):
    any_spec = pl.BlockSpec(memory_space=pl.ANY)
    out = jax.ShapeDtypeStruct((ROWS, D), BF16)
    rising, falling, perm = pl.pallas_call(
        kernel,
        out_shape=(out, out, jax.ShapeDtypeStruct((2, ROWS, 128), BF16)),
        in_specs=[any_spec] * 9,
        out_specs=(any_spec, any_spec, any_spec),
        scratch_shapes=[
            pltpu.VMEM((128, D), BF16),
            pltpu.VMEM((128, D), BF16),
            pltpu.VMEM((1, D), BF16),
            pltpu.VMEM((2, D), BF16),
            pltpu.VMEM((2, 1, ROWS), jnp.int32),
            pltpu.VMEM((8, ROWS, D), BF16),
            pltpu.VMEM((ROWS, D), BF16),
            pltpu.VMEM((2, D, HID), BF16),
            pltpu.VMEM((2, D, HID), BF16),
            pltpu.VMEM((4, HID, HALF), BF16),
            pltpu.VMEM((8 * ROWS, 2 * HID), BF16),
            pltpu.VMEM((8 * ROWS, 2 * HID), BF16),
            pltpu.VMEM((2 * ROWS, 4 * HID), F32),
            pltpu.VMEM((4 * ROWS, HALF), BF16),
            pltpu.VMEM((4 * ROWS, HALF), BF16),
            pltpu.VMEM((2 * ROWS, HALF), BF16),
            pltpu.VMEM((ROWS, HALF), BF16),
            pltpu.VMEM((ROWS, HALF), BF16),
            pltpu.VMEM((2 * ROWS, HALF), BF16),
            pltpu.VMEM((2, 2 * ROWS, HALF), BF16),
            pltpu.VMEM((2, ROWS, HALF), BF16),
            pltpu.VMEM((128, 128), BF16),
            pltpu.VMEM((2, ROWS, 128), BF16),
            pltpu.VMEM((128, 128), F32),
            pltpu.SemaphoreType.DMA((9,)),
            pltpu.SemaphoreType.DMA((N_SEM,)),
            pltpu.SemaphoreType.DMA((N_SEM,)),
            pltpu.SemaphoreType.REGULAR,
        ],
        compiler_params=pltpu.CompilerParams(
            collective_id=0, has_side_effects=True, vmem_limit_bytes=60 * 2**20
        ),
        name="relay",
    )(
        stream_up[0], stream_down[0], norm_gain, router[0].T, w_gate[0], w_up[0], w_down[0],
        routes_up.reshape(1, ROWS), routes_down.reshape(1, ROWS),
    )
    rising, falling = pl.pallas_call(
        reorder,
        out_shape=(out, out),
        in_specs=[any_spec] * 3,
        out_specs=(any_spec, any_spec),
        scratch_shapes=[
            pltpu.VMEM((2, ROWS, 128), BF16),
            pltpu.VMEM((2, ROWS, D), BF16),
            pltpu.VMEM((2, ROWS, D), BF16),
            pltpu.SemaphoreType.DMA((1 + 4 * NK,)),
        ],
        compiler_params=pltpu.CompilerParams(vmem_limit_bytes=60 * 2**20),
        name="reorder",
    )(rising, falling, perm)
    return rising[None], falling[None]


def solution(mesh):
    placed = (
        P("pp", "ep", None),
        P("pp", "ep", None),
        P("pp", None),
        P("pp", None, None),
        P("pp", None, "ep"),
        P("pp", None, "ep"),
        P("pp", "ep", None),
        P(None, "pp", "ep", None),
        P(None, "pp", "ep", None),
    )
    return jax.shard_map(
        local,
        mesh=mesh,
        in_specs=placed,
        out_specs=(P("pp", "ep", None), P("pp", "ep", None)),
        check_vma=False,
    )
```

time: 171 us -> 137 us (0.80); the launches traced: 168 us -> 137 us
  Pallas kernels: 160 us -> 137 us
  local copies, waits for them, and re-layouts: 7.2 us -> 0 us
    pallas_call x1 -> x2, Pallas kernels: 160 us -> 137 us  [the longest x1 132 us: local(): pl.pallas_call(kernel, out_shape=(out, out, jax.ShapeDtypeStruct((2, ROWS...]
    unnamed x12 -> x0, local copies, waits for them, and re-layouts: 7.2 us -> none
where the time goes in v3:
time: 137 us
  Pallas kernels  137 us (100%)
    pallas_call x1, Pallas kernels, local(): pl.pallas_call(kernel, out_shape=(out, out, jax.ShapeDtypeStruct((2, ROWS...  132 us
    pallas_call x1, Pallas kernels, local(): pl.pallas_call(reorder, out_shape=(out, out), in_specs=[any_spec] * 3, ou...  4.19 us

profile of v3, /device:TPU:2, one launch (start us, length us, event | category | flops | bytes accessed | tf_op | source)
XLA Modules:
  0.0 137.2 jit_solution(3993617003481165066)
XLA Ops:
  0.6 132.4 %relay.1 = (bf16[64,7168]{1,0:T(8,128)(2,1)}, bf16[64,7168]{1,0:T(8,128)(2,1)}, bf16[2,64,128]{2,1,0:T(8,128)(2,1)}) custom-call(bf16[64,7168]{1,0:T(8,128)(2,1)} %bitcast.15, bf16[64,7168]{1,0:T(8,128)(2,1)} %bitcast.16, bf16[1,7168]{1,0:T(2,128)(2,1)} %gain_ref.1, bf16[2,7168]{1,0:T(2,128)(2,1)} %bitcast.17, bf16[7168,128]{1,0:T(8,128)(2,1)} %bitcast.12, ...), custom_call_target="tpu_custom_call" | custom-call | tf_op jit(solution)/shard_map/relay/pallas_call | solution.py:718
  133.0 4.2 %reorder.1 = (bf16[64,7168]{1,0:T(8,128)(2,1)}, bf16[64,7168]{1,0:T(8,128)(2,1)}) custom-call(bf16[64,7168]{1,0:T(8,128)(2,1)} %get-tuple-element.7.up_ref, bf16[64,7168]{1,0:T(8,128)(2,1)} %get-tuple-element.8.down_ref, bf16[2,64,128]{2,1,0:T(8,128)(2,1)} %get-tuple-element.9.perm_ref), custom_call_target="tpu_custom_call" | custom-call | tf_op jit(solution)/shard_map/reorder/pallas_call | solution.py:761

commit v4 on v3

--- a/solution.py
+++ b/solution.py
@@ -21,14 +21,15 @@
 NJ = HALF // JC
 NB = NJ - 2
 NR = NB + 4
+WD_FIRST = 64
 KX = 3
 
 OWN, Z_OWN, ENT, Z_ENT, X_OWN, D_OWN, X_ENT, D_ENT = range(8)
 
 OWN_X, OWN_Z, CROSS, ENT_X, ENT_Z, FWD_OWN, FWD_ENT = range(0, 7 * NK, NK)
 W_BASE = 7 * NK
-WD_Z, WD_RELAY, WD_CORE, WG_CORE, WU_CORE = range(W_BASE, W_BASE + 5)
-ACT_Z = W_BASE + 5
+WD_Z, WD_Z_MORE, WD_RELAY, WD_CORE, WG_CORE, WU_CORE = range(W_BASE, W_BASE + 6)
+ACT_Z = W_BASE + 6
 R_BASE = ACT_Z + 4
 RET_XO, RET_XE, RET_ZO, RET_ZC, RET_C = range(R_BASE, R_BASE + 5 * NR, NR)
 OUT_UP = R_BASE + 5 * NR
@@ -120,7 +121,9 @@
 
     half_mine = pl.ds(pl.multiple_of(my_half, HALF), HALF)
     half_other = pl.ds(pl.multiple_of(other_half, HALF), HALF)
-    wd_z = remote(wd_ref.at[:, half_other], wd.at[2], WD_Z, zn)
+    some, more = pl.ds(0, WD_FIRST), pl.ds(WD_FIRST, HID - WD_FIRST)
+    wd_z = remote(wd_ref.at[some, half_other], wd.at[2, some], WD_Z, zn)
+    wd_z_more = remote(wd_ref.at[more, half_other], wd.at[2, more], WD_Z_MORE, zn)
     wd_relay = remote(wd.at[2], wd.at[3], WD_RELAY, core)
     wd_core = remote(wd_ref.at[:, half_mine], wd.at[1], WD_CORE, core)
     wg_core = remote(wg_ref, wg.at[1], WG_CORE, core)
@@ -279,17 +282,13 @@
         def _():
             pl.semaphore_signal(barrier, inc=1, device_id=to, device_id_type=MESH)
 
-    load_wg.start()
-    load_wu.start()
-    load_wd.start()
 
     token_r = lax.broadcasted_iota(jnp.int32, (128, 128), 0)
     token_c = lax.broadcasted_iota(jnp.int32, (128, 128), 1)
     load_routes(0, routes_up).wait()
     load_routes(1, routes_down).wait()
-    wide_0 = dot(routes_vm[0].astype(F32), jnp.where(token_r[:64] == token_c[:64], 1.0, 0.0))
-    wide_1 = dot(routes_vm[1].astype(F32), jnp.where(token_r[:64] + 64 == token_c[:64], 1.0, 0.0))
-    chosen = jnp.broadcast_to((wide_0 + wide_1).astype(jnp.int32), (128, 128))
+    chosen = jnp.concatenate([routes_vm[0], routes_vm[1]], axis=1)
+    chosen = jnp.broadcast_to(chosen, (128, 128))
     mine = (chosen == expert).astype(F32)
     before = ((token_r < token_c) & (token_r // 64 == token_c // 64)).astype(F32)
     ahead = dot(mine.astype(BF16), before.astype(BF16))
@@ -298,14 +297,22 @@
     target = stream + jnp.where(mine > 0.5, ahead, 64.0 + inside - ahead)
     hit = (token_r.astype(F32) == target).astype(F32)
     place[...] = hit.astype(BF16)
-    back_to = stream * 2.0 + jnp.where(mine > 0.5, ahead, 32.0 + inside - ahead)
-    back_hit = (token_r.astype(F32) == back_to).astype(F32).T.astype(BF16)
-    perm[...] = jnp.zeros_like(perm)
-    perm[0, :, 0:ROWS] = back_hit[:ROWS, :ROWS]
-    perm[1, :, 0:ROWS] = back_hit[ROWS:, ROWS:]
-
+    pl.semaphore_wait(barrier, len(near) + lower)
+    for step in steps:
+        to = section(step)
+
+        @pl.when(to[0] < pp)
+        def _():
+            pl.semaphore_signal(ready, inc=1, device_id=to, device_id_type=MESH)
+
+    wd_z.start()
     load_x(0, up_ref).wait()
     load_x(1, down_ref).wait()
+    for copy in (wg_core, wu_core, wd_core, load_wg, load_wu, load_wd):
+        copy.start()
+
+    load_gain.wait()
+    load_router.wait()
 
     def squares(k, total):
         part = xin[:, cols(k)].astype(F32)
@@ -322,17 +329,6 @@
     def normed(k):
         gain = gain_vm[:, cols(k)].astype(F32)
         return (xin[:, cols(k)].astype(F32) * weight[:, 0:1] * gain).astype(BF16)
-
-    load_gain.wait()
-    load_router.wait()
-    pl.semaphore_wait(barrier, len(near) + lower)
-    for step in steps:
-        to = section(step)
-
-        @pl.when(to[0] < pp)
-        def _():
-            pl.semaphore_signal(ready, inc=1, device_id=to, device_id_type=MESH)
-
 
     def first(k):
         moved = dot(place[...], normed(k)).astype(BF16)
@@ -343,9 +339,12 @@
         own_z(k).start()
 
     loop(NK, first)
-    wg_core.start()
-    wu_core.start()
-    wd_core.start()
+
+    back_to = stream * 2.0 + jnp.where(mine > 0.5, ahead, 32.0 + inside - ahead)
+    back_hit = (token_r.astype(F32) == back_to).astype(F32).T.astype(BF16)
+    perm[...] = jnp.zeros_like(perm)
+    perm[0, :, 0:ROWS] = back_hit[:ROWS, :ROWS]
+    perm[1, :, 0:ROWS] = back_hit[ROWS:, ROWS:]
 
     def affinity(k, carry):
         own, foreign = carry
@@ -394,7 +393,7 @@
         hidden_step(0, k)
 
     loop(NK, second)
-    wd_z.start()
+    wd_z_more.start()
 
     @pl.when(lower < len(steps))
     def _():
@@ -432,6 +431,7 @@
 
     loop(NK, relay)
     wd_z.wait_recv()
+    wd_z_more.wait_recv()
     wd_relay.start()
     wd_core.wait_recv()
 
@@ -634,7 +634,7 @@
     final_e(*second[1])
     final_o(*second[1])
 
-    for copy in (wd_z, wd_relay, wd_core, wg_core, wu_core, act_z(0), act_z(1), act_z(2), act_z(3)):
+    for copy in (wd_z, wd_z_more, wd_relay, wd_core, wg_core, wu_core, act_z(0), act_z(1), act_z(2), act_z(3)):
         copy.wait_send()
     by_stream(lambda s: perm_up(s).wait(), lambda s: perm_dn(s).wait())
 
@@ -692,19 +692,19 @@
     load_perm = pltpu.make_async_copy(perm_ref, perm, sem.at[0])
     load_perm.start()
     loads, stores = [], []
-    for k in range(0, D, KC):
-        cols = pl.ds(k, KC)
+    for k in range(0, D, HALF):
+        cols = pl.ds(k, HALF)
         for stream, (src, dst) in enumerate(((up_ref, out_up), (down_ref, out_down))):
             n = len(loads)
             held = rows.at[stream, :, cols]
             loads.append(pltpu.make_async_copy(src.at[:, cols], held, sem.at[1 + n]))
             done = outs.at[stream, :, cols]
-            stores.append(pltpu.make_async_copy(done, dst.at[:, cols], sem.at[1 + 2 * NK + n]))
+            stores.append(pltpu.make_async_copy(done, dst.at[:, cols], sem.at[1 + 4 + n]))
     for load in loads:
         load.start()
     load_perm.wait()
     for n, (load, store) in enumerate(zip(loads, stores)):
-        stream, cols = n % 2, pl.ds(n // 2 * KC, KC)
+        stream, cols = n % 2, pl.ds(n // 2 * HALF, HALF)
         load.wait()
         outs[stream, :, cols] = dot(perm[stream, :, 0:ROWS], rows[stream, :, cols]).astype(BF16)
         store.start()
@@ -767,7 +767,7 @@
             pltpu.VMEM((2, ROWS, 128), BF16),
             pltpu.VMEM((2, ROWS, D), BF16),
             pltpu.VMEM((2, ROWS, D), BF16),
-            pltpu.SemaphoreType.DMA((1 + 4 * NK,)),
+            pltpu.SemaphoreType.DMA((1 + 8,)),
         ],
         compiler_params=pltpu.CompilerParams(vmem_limit_bytes=60 * 2**20),
         name="reorder",

time: 137 us -> 136 us (level)
  Pallas kernels: 137 us -> 135 us
where the time goes in v4:
time: 136 us
  Pallas kernels  135 us (99%)
    pallas_call x1, Pallas kernels, local(): pl.pallas_call(kernel, out_shape=(out, out, jax.ShapeDtypeStruct((2, ROWS...  132 us
    pallas_call x1, Pallas kernels, local(): pl.pallas_call(reorder, out_shape=(out, out), in_specs=[any_spec] * 3, ou...  2.96 us

profile of v4, /device:TPU:2, one launch (start us, length us, event | category | flops | bytes accessed | tf_op | source)
XLA Modules:
  0.0 135.9 jit_solution(16886085170425370962)
XLA Ops:
  0.6 132.3 %relay.1 = (bf16[64,7168]{1,0:T(8,128)(2,1)}, bf16[64,7168]{1,0:T(8,128)(2,1)}, bf16[2,64,128]{2,1,0:T(8,128)(2,1)}) custom-call(bf16[64,7168]{1,0:T(8,128)(2,1)} %bitcast.15, bf16[64,7168]{1,0:T(8,128)(2,1)} %bitcast.16, bf16[1,7168]{1,0:T(2,128)(2,1)} %gain_ref.1, bf16[2,7168]{1,0:T(2,128)(2,1)} %bitcast.17, bf16[7168,128]{1,0:T(8,128)(2,1)} %bitcast.12, ...), custom_call_target="tpu_custom_call" | custom-call | tf_op jit(solution)/shard_map/relay/pallas_call | solution.py:718
  132.9 3.0 %reorder.1 = (bf16[64,7168]{1,0:T(8,128)(2,1)}, bf16[64,7168]{1,0:T(8,128)(2,1)}) custom-call(bf16[64,7168]{1,0:T(8,128)(2,1)} %get-tuple-element.7.up_ref, bf16[64,7168]{1,0:T(8,128)(2,1)} %get-tuple-element.8.down_ref, bf16[2,64,128]{2,1,0:T(8,128)(2,1)} %get-tuple-element.9.perm_ref), custom_call_target="tpu_custom_call" | custom-call | tf_op jit(solution)/shard_map/reorder/pallas_call | solution.py:761

commit v5 on v4

--- a/solution.py
+++ b/solution.py
@@ -193,7 +193,7 @@
         return moved(out_src(q, stream, at), out_dst(out_dn, q, at), index, index, below)
 
     def turn(j, q):
-        return jnp.where((j >= NB) & (q >= 2), 3, lax.rem(j + q, 4))
+        return jnp.where((j >= NB) & (q >= 2), 3, lax.rem(j + q + 3, 4))
 
     def via_at(q, at):
         return via.at[q % 2, row_at(q), pl.ds(at, JC)]
@@ -517,7 +517,7 @@
         finish(j, at, 3, fz[span(streams, ROWS, 32), pl.ds(at, JC)].astype(F32), streams)
 
     def relays(j):
-        return lax.rem(yi + 4 * NJ - j, 4), lax.rem(3 - yi + 4 * NJ - j, 4)
+        return lax.rem(yi + 4 * NJ - j - 3, 4), lax.rem(3 - yi + 4 * NJ - j - 3, 4)
 
     def pass_on(kind, p, j, at, streams):
         up, dn = relays(j)
@@ -591,12 +591,13 @@
             for part in first:
                 sums_o(*part)
 
+        sums_e(*piece(i))
+
         @pl.when(i + 3 < NB)
         def _():
             sums_o(*piece(i + 3))
 
         final_o(*piece(i))
-        sums_e(*piece(i))
 
         @pl.when(i >= 1)
         def _():

time: 136 us -> 136 us (level)
  no operation moved by 1% of the time
where the time goes in v5:
time: 136 us; the launch traced here: 135 us
  Pallas kernels  135 us (99%)
    pallas_call x1, Pallas kernels, local(): pl.pallas_call(kernel, out_shape=(out, out, jax.ShapeDtypeStruct((2, ROWS...  132 us
    pallas_call x1, Pallas kernels, local(): pl.pallas_call(reorder, out_shape=(out, out), in_specs=[any_spec] * 3, ou...  2.94 us

profile of v5, /device:TPU:2, one launch (start us, length us, event | category | flops | bytes accessed | tf_op | source)
XLA Modules:
  0.0 135.3 jit_solution(9093255321344507282)
XLA Ops:
  0.6 131.7 %relay.1 = (bf16[64,7168]{1,0:T(8,128)(2,1)}, bf16[64,7168]{1,0:T(8,128)(2,1)}, bf16[2,64,128]{2,1,0:T(8,128)(2,1)}) custom-call(bf16[64,7168]{1,0:T(8,128)(2,1)} %bitcast.15, bf16[64,7168]{1,0:T(8,128)(2,1)} %bitcast.16, bf16[1,7168]{1,0:T(2,128)(2,1)} %gain_ref.1, bf16[2,7168]{1,0:T(2,128)(2,1)} %bitcast.17, bf16[7168,128]{1,0:T(8,128)(2,1)} %bitcast.12, ...), custom_call_target="tpu_custom_call" | custom-call | tf_op jit(solution)/shard_map/relay/pallas_call | solution.py:719
  132.3 2.9 %reorder.1 = (bf16[64,7168]{1,0:T(8,128)(2,1)}, bf16[64,7168]{1,0:T(8,128)(2,1)}) custom-call(bf16[64,7168]{1,0:T(8,128)(2,1)} %get-tuple-element.7.up_ref, bf16[64,7168]{1,0:T(8,128)(2,1)} %get-tuple-element.8.down_ref, bf16[2,64,128]{2,1,0:T(8,128)(2,1)} %get-tuple-element.9.perm_ref), custom_call_target="tpu_custom_call" | custom-call | tf_op jit(solution)/shard_map/reorder/pallas_call | solution.py:762
